TPU v7x, 32 devices: a whole 2x2x4 slice. The times are simulated.
32 devices in a mesh: dp: 8 (over y, x, core), seq: 4 (over z).
Axes of the slice: x: 2, y: 2, z: 4, core: 2. Of those that a mesh axis runs over, the one named last changes fastest.
Arguments:
- enc_input: bfloat16 [32, 1024, 512], P('dp', 'seq'), may hold values from -6 to 6
- dec_input: bfloat16 [32, 100, 512], P('dp', 'seq'), may hold values from -6 to 6
- targets: float32 [32, 100, 14], P('dp', 'seq'), may hold values from -6 to 6
- lengths: int32 [32], P('dp'), may hold values from 1 to 100, as said below
- attention_mats: float32 [12, 512, 512], P(None, ('dp', 'seq')), may hold values from -1.8856181 to 1.8856181
- expand_mats: float32 [2, 512, 3200], P(None, ('dp', 'seq')), may hold values from -0.25 to 0.25
- reduce_mats: float32 [2, 3200, 512], P(None, None, ('dp', 'seq')), may hold values from -0.109375 to 0.109375
- action_head: float32 [512, 14], P(('dp', 'seq')), may hold values from -0.25 to 0.25
- query_pos: float32 [100, 512], P(None, ('dp', 'seq')), may hold values from -3 to 3
- vectors: float32 [21, 512], P(None, ('dp', 'seq')), may hold values from -1.2 to 1.4, as said below
- expand_bias: float32 [6400], P(('dp', 'seq')), may hold values from -1 to 1
- first_attention: float32 [12, 512, 512], P(None, ('dp', 'seq')), may hold values from -0.875 to 0.875
- first_expand: float32 [2, 512, 3200], P(None, ('dp', 'seq')), may hold values from -0.875 to 0.875
- first_reduce: float32 [2, 3200, 512], P(None, None, ('dp', 'seq')), may hold values from -0.875 to 0.875
- first_head: float32 [512, 14], P(('dp', 'seq')), may hold values from -3.5 to 3.5
- first_query: float32 [100, 512], P(None, ('dp', 'seq')), may hold values from -0.01953125 to 0.01953125
- first_vectors: float32 [21, 512], P(None, ('dp', 'seq')), may hold values from -1.75 to 1.75
- first_bias: float32 [6400], P(('dp', 'seq')), may hold values from -0.4375 to 0.4375
- second_attention: float32 [12, 512, 512], P(None, ('dp', 'seq')), may hold values from 0.00016 to 0.00256
- second_expand: float32 [2, 512, 3200], P(None, ('dp', 'seq')), may hold values from 0.00016 to 0.00256
- second_reduce: float32 [2, 3200, 512], P(None, None, ('dp', 'seq')), may hold values from 0.00016 to 0.00256
- second_head: float32 [512, 14], P(('dp', 'seq')), may hold values from 0.00256 to 0.04096
- second_query: float32 [100, 512], P(None, ('dp', 'seq')), may hold values from 6.4e-08 to 1.024e-06
- second_vectors: float32 [21, 512], P(None, ('dp', 'seq')), may hold values from 0.00064 to 0.01024
- second_bias: float32 [6400], P(('dp', 'seq')), may hold values from 4e-05 to 0.00064
Outputs:
- enc_input_grad: bfloat16 [32, 1024, 512], P('dp', 'seq')
- dec_input_grad: bfloat16 [32, 100, 512], P('dp', 'seq')
- first_attention_new: float32 [12, 512, 512], P(None, ('dp', 'seq'))
- second_attention_new: float32 [12, 512, 512], P(None, ('dp', 'seq'))
- attention_master: float32 [12, 512, 512], P(None, ('dp', 'seq'))
- attention_half: bfloat16 [12, 512, 512], P(None, ('dp', 'seq'))
- first_expand_new: float32 [2, 512, 3200], P(None, ('dp', 'seq'))
- second_expand_new: float32 [2, 512, 3200], P(None, ('dp', 'seq'))
- expand_master: float32 [2, 512, 3200], P(None, ('dp', 'seq'))
- expand_half: bfloat16 [2, 512, 3200], P(None, ('dp', 'seq'))
- first_reduce_new: float32 [2, 3200, 512], P(None, None, ('dp', 'seq'))
- second_reduce_new: float32 [2, 3200, 512], P(None, None, ('dp', 'seq'))
- reduce_master: float32 [2, 3200, 512], P(None, None, ('dp', 'seq'))
- reduce_half: bfloat16 [2, 3200, 512], P(None, None, ('dp', 'seq'))
- first_head_new: float32 [512, 14], P(('dp', 'seq'))
- second_head_new: float32 [512, 14], P(('dp', 'seq'))
- head_master: float32 [512, 14], P(('dp', 'seq'))
- head_half: bfloat16 [512, 14], P(('dp', 'seq'))
- first_query_new: float32 [100, 512], P(None, ('dp', 'seq'))
- second_query_new: float32 [100, 512], P(None, ('dp', 'seq'))
- query_master: float32 [100, 512], P(None, ('dp', 'seq'))
- query_half: bfloat16 [100, 512], P(None, ('dp', 'seq'))
- first_vectors_new: float32 [21, 512], P(None, ('dp', 'seq'))
- second_vectors_new: float32 [21, 512], P(None, ('dp', 'seq'))
- vectors_master: float32 [21, 512], P(None, ('dp', 'seq'))
- vectors_half: bfloat16 [21, 512], P(None, ('dp', 'seq'))
- first_bias_new: float32 [6400], P(('dp', 'seq'))
- second_bias_new: float32 [6400], P(('dp', 'seq'))
- bias_master: float32 [6400], P(('dp', 'seq'))
- bias_half: bfloat16 [6400], P(('dp', 'seq'))
Inputs may be any that keep to these rules, and one draw needn't show every extreme that they name: `lengths`: in each aligned group of 4 items one item has all 100 steps valid. `vectors`: rows 3, 6, 11, 16 and 19 are LayerNorm gains, the other rows biases and shifts.
All inputs are finite; a program needn't handle non-finite values.
Results may differ from a plain program's by a relative error of at most 0.02.
Values may be sent and summed in bfloat16 or wider, within the bound.
No kernel may reach another device: no remote copies, remote signals or barrier semaphores. Data moves between devices by JAX's collectives and lax.ppermute only.
A program may use at most 256 MiB of HBM per device.

v0:
```python
import functools
import math

import jax
import jax.numpy as jnp
import numpy as np
from jax import lax
from jax.experimental import pallas as pl
from jax.experimental.pallas import tpu as pltpu
from jax.sharding import PartitionSpec as P

HEADS = 8
HDIM = 64
PAIR = 2 * HDIM
STEP = 10
ALL = ("dp", "seq")

beta_first = 0.9
beta_second = 0.999
epsilon = 1e-08
decay_rate = 0.1
rate_matrix = 0.08
rate_vector = 0.2

BF = jnp.bfloat16
F32 = jnp.float32
MB = 1 << 20
SCALE = HDIM ** (-0.5)


def to_half(values):
    return values.astype(BF)


def mm(a, b):
    return lax.dot_general(a, b, (((1,), (0,)), ((), ())), preferred_element_type=F32)


def mm_t(a, b):
    return lax.dot_general(a, b, (((1,), (1,)), ((), ())), preferred_element_type=F32)


def column_sum(values):
    return jnp.sum(values.astype(F32), axis=0, keepdims=True)


def norm_parts(values):
    center = values - jnp.mean(values, axis=-1, keepdims=True)
    scale = lax.rsqrt(jnp.mean(center * center, axis=-1, keepdims=True) + 1e-05)
    return center * scale, scale


def layer_norm(values, gain, shift):
    return norm_parts(values)[0] * gain + shift


def norm_back(values, gain, gradient):
    unit, scale = norm_parts(values)
    inner = gradient * gain
    mean_inner = jnp.mean(inner, axis=-1, keepdims=True)
    mean_cross = jnp.mean(inner * unit, axis=-1, keepdims=True)
    back = scale * (inner - mean_inner - unit * mean_cross)
    return back, column_sum(gradient * unit), column_sum(gradient)


GELU_A = math.sqrt(2.0 / math.pi)
GELU_B = 0.044715


def gelu_parts(u):
    square = u * u
    bend = jnp.tanh(u * (GELU_A + GELU_A * GELU_B * square))
    half = 0.5 + 0.5 * bend
    slope = half + (0.5 * u) * (1.0 - bend * bend) * (GELU_A + 3.0 * GELU_A * GELU_B * square)
    return u * half, slope


def gelu(u):
    return u * (0.5 + 0.5 * jnp.tanh(u * (GELU_A + GELU_A * GELU_B * (u * u))))


def sine_table(count, width):
    halves = np.arange(width // 2, dtype=np.float64)
    frequency = np.exp(halves * (-2.0 * math.log(10000.0) / width))
    angles = np.arange(count)[:, None] * frequency[None, :]
    table = np.stack([np.sin(angles), np.cos(angles)], axis=-1).reshape(count, width)
    return table.astype(np.float32)


def own_lanes(values, h):
    lane = lax.broadcasted_iota(jnp.int32, values.shape, 1)
    return jnp.where((lane < HDIM) == (h == 0), values, jnp.zeros_like(values))


def join_rows(first, second):
    row = lax.broadcasted_iota(jnp.int32, first.shape, 0)
    return jnp.where(row < HDIM, first, second)


def settle_kernel(top_ref, bottom_ref, turn_ref, out_ref):
    cut = top_ref.shape[0]
    out_ref[...] = to_half(mm(turn_ref[:, :cut], top_ref[...]) + mm(turn_ref[:, cut:], bottom_ref[...]))


def settle(top, bottom, turn, block):
    cut, columns = top.shape
    part = pl.BlockSpec((cut, block), lambda i: (0, i))
    return pl.pallas_call(
        settle_kernel,
        grid=(columns // block,),
        in_specs=[part, part, pl.BlockSpec(turn.shape, lambda i: (0, 0))],
        out_specs=pl.BlockSpec((2 * cut, block), lambda i: (0, i)),
        out_shape=jax.ShapeDtypeStruct((2 * cut, columns), BF),
        compiler_params=pltpu.CompilerParams(vmem_limit_bytes=40 * MB),
        cost_estimate=pl.CostEstimate(flops=8 * cut * cut * columns, bytes_accessed=8 * cut * columns, transcendentals=0),
        name="settle",
    )(top, bottom, turn)


def attend_kernel(
    x_ref, pos_ref, wq_ref, wk_ref, wv_ref, vec_ref, q_ref, k_ref, v_ref, o_ref, log_ref, in_ref, vt_ref, *, chunk
):
    @pl.when(pl.program_id(0) == 0)
    def _():
        in_ref[...] = to_half(x_ref[...].astype(F32) + pos_ref[...])

    q_ref[...] = to_half(mm(in_ref[...], wq_ref[...]) + vec_ref[0:1, :])
    k_ref[...] = to_half(mm(in_ref[...], wk_ref[...]))
    values = to_half(mm(x_ref[...], wv_ref[...]) + vec_ref[1:2, :])
    v_ref[...] = values
    vt_ref[...] = values.T

    def step(i, carry):
        at = pl.ds(i * chunk, chunk)
        query = q_ref[at, :] * BF(SCALE)
        mixed = []
        for h in range(2):
            scores = mm_t(k_ref[...], own_lanes(query, h))
            peak = jnp.max(scores, axis=0, keepdims=True)
            weights = jnp.exp(scores - peak)
            total = jnp.sum(weights, axis=0, keepdims=True)
            mixed.append(mm(vt_ref[...], to_half(weights)) / total)
            log_ref[0, pl.ds(h, 1), at] = peak + jnp.log(total)
        o_ref[at, :] = to_half(join_rows(*mixed).T)
        return carry

    lax.fori_loop(0, q_ref.shape[0] // chunk, step, 0)


def attend(x, positions, weights, vec):
    rows, width = x.shape
    pairs = width // PAIR
    whole = pl.BlockSpec((rows, width), lambda i: (0, 0))
    own = pl.BlockSpec((rows, PAIR), lambda i: (0, i))
    mats = [pl.BlockSpec((width, PAIR), lambda i, j=j: (0, i + j * pairs)) for j in range(3)]
    half = jax.ShapeDtypeStruct((rows, width), BF)
    return pl.pallas_call(
        functools.partial(attend_kernel, chunk=256),
        grid=(pairs,),
        in_specs=[whole, whole] + mats + [pl.BlockSpec((vec.shape[0], PAIR), lambda i: (0, i))],
        out_specs=[own] * 4 + [pl.BlockSpec((1, 2, rows), lambda i: (i, 0, 0))],
        out_shape=[half] * 4 + [jax.ShapeDtypeStruct((pairs, 2, rows), F32)],
        scratch_shapes=[pltpu.VMEM((rows, width), BF), pltpu.VMEM((PAIR, rows), BF)],
        compiler_params=pltpu.CompilerParams(vmem_limit_bytes=56 * MB),
        cost_estimate=pl.CostEstimate(
            flops=16 * rows * rows * width, bytes_accessed=12 * rows * width, transcendentals=8 * rows * rows
        ),
        name="attend",
    )(x, positions, weights, weights, weights, vec)


def forward_kernel(
    mixed_ref, x_ref, out_ref, vec_ref, e_ref, r_ref, bias_ref,
    sum_one_ref, hidden_ref, u_ref, sum_two_ref, memory_ref, *, tile
):
    step = pl.program_id(0)
    count = x_ref.shape[0] // tile

    def rows_of(i):
        return pl.ds(pl.multiple_of(i * tile, tile), tile)

    @pl.when(step == 0)
    def _():
        def body(i, carry):
            at = rows_of(i)
            total = x_ref[at, :].astype(F32) + mm(mixed_ref[at, :], out_ref[...]) + vec_ref[2:3, :]
            sum_one_ref[at, :] = total
            hidden = layer_norm(total, vec_ref[3:4, :], vec_ref[4:5, :])
            hidden_ref[at, :] = to_half(hidden)
            sum_two_ref[at, :] = hidden + vec_ref[5:6, :]
            return carry

        lax.fori_loop(0, count, body, 0)

    def body(i, carry):
        at = rows_of(i)
        u = mm(hidden_ref[at, :], e_ref[...]) + bias_ref[...]
        u_ref[at, :] = u
        sum_two_ref[at, :] += mm_t(to_half(gelu(u)), r_ref[...])
        return carry

    lax.fori_loop(0, count, body, 0)

    @pl.when(step == pl.num_programs(0) - 1)
    def _():
        def body(i, carry):
            at = rows_of(i)
            memory_ref[at, :] = layer_norm(sum_two_ref[at, :], vec_ref[6:7, :], vec_ref[7:8, :])
            return carry

        lax.fori_loop(0, count, body, 0)


def feed_forward(mixed, x, enc_mats, vec, enc_ffn, bias):
    rows, width = x.shape
    width_ff = bias.shape[1]
    block = 640 if width_ff % 640 == 0 else width_ff
    steps = width_ff // block
    whole = pl.BlockSpec((rows, width), lambda i: (0, 0))
    float_rows = jax.ShapeDtypeStruct((rows, width), F32)
    return pl.pallas_call(
        functools.partial(forward_kernel, tile=256),
        grid=(steps,),
        in_specs=[
            whole,
            whole,
            pl.BlockSpec((width, width), lambda i: (0, 3)),
            pl.BlockSpec(vec.shape, lambda i: (0, 0)),
            pl.BlockSpec((width, block), lambda i: (0, i)),
            pl.BlockSpec((width, block), lambda i: (0, i + steps)),
            pl.BlockSpec((1, block), lambda i: (0, i)),
        ],
        out_specs=[whole, whole, pl.BlockSpec((rows, block), lambda i: (0, i)), whole, whole],
        out_shape=[
            float_rows,
            jax.ShapeDtypeStruct((rows, width), BF),
            jax.ShapeDtypeStruct((rows, width_ff), F32),
            float_rows,
            float_rows,
        ],
        compiler_params=pltpu.CompilerParams(vmem_limit_bytes=56 * MB),
        cost_estimate=pl.CostEstimate(
            flops=4 * rows * width * width_ff, bytes_accessed=4 * rows * width_ff, transcendentals=rows * width_ff
        ),
        name="feed_forward",
    )(mixed, x, enc_mats, vec, enc_ffn, enc_ffn, bias)


def turned(turn, values):
    return to_half(mm_t(turn, values))


def lefts_kernel(x_ref, pos_ref, mixed_ref, hidden_ref, turn_ref, in_t_ref, x_t_ref, mixed_t_ref, hidden_t_ref):
    in_t_ref[...] = turned(turn_ref[...], to_half(x_ref[...].astype(F32) + pos_ref[...]))
    x_t_ref[...] = turned(turn_ref[...], x_ref[...])
    mixed_t_ref[...] = turned(turn_ref[...], mixed_ref[...])
    hidden_t_ref[...] = turned(turn_ref[...], hidden_ref[...])


def lefts(x, positions, mixed, hidden, turn):
    rows, width = x.shape
    return pl.pallas_call(
        lefts_kernel,
        out_shape=[jax.ShapeDtypeStruct((width, rows), BF)] * 4,
        compiler_params=pltpu.CompilerParams(vmem_limit_bytes=40 * MB),
        cost_estimate=pl.CostEstimate(flops=8 * rows * width * width, bytes_accessed=20 * rows * width, transcendentals=0),
        name="lefts",
    )(x, positions, mixed, hidden, turn)


def norm_kernel(grad_ref, sum_two_ref, vec_ref, turn_ref, two_ref, half_t_ref, vec_grad_ref, half_ref, *, tile):
    vec_grad_ref[...] = jnp.zeros_like(vec_grad_ref)

    def body(i, carry):
        at = pl.ds(pl.multiple_of(i * tile, tile), tile)
        back, gain, shift = norm_back(sum_two_ref[at, :], vec_ref[6:7, :], grad_ref[at, :])
        two_ref[at, :] = back
        half_ref[at, :] = to_half(back)
        vec_grad_ref[0:1, :] += column_sum(back)
        vec_grad_ref[1:2, :] += gain
        vec_grad_ref[2:3, :] += shift
        return carry

    lax.fori_loop(0, grad_ref.shape[0] // tile, body, 0)
    half_t_ref[...] = turned(turn_ref[...], half_ref[...])


def last_norm_back(grad, sum_two, vec, turn):
    rows, width = grad.shape
    return pl.pallas_call(
        functools.partial(norm_kernel, tile=256),
        out_shape=[
            jax.ShapeDtypeStruct((rows, width), F32),
            jax.ShapeDtypeStruct((width, rows), BF),
            jax.ShapeDtypeStruct((8, width), F32),
        ],
        scratch_shapes=[pltpu.VMEM((rows, width), BF)],
        compiler_params=pltpu.CompilerParams(vmem_limit_bytes=40 * MB),
        cost_estimate=pl.CostEstimate(flops=2 * rows * width * width, bytes_accessed=14 * rows * width, transcendentals=0),
        name="last_norm_back",
    )(grad, sum_two, vec, turn)


def backward_kernel(
    grad_ref, half_t_ref, sum_one_ref, hidden_t_ref, mixed_t_ref, u_ref, e_ref, r_ref, out_ref, vec_ref,
    keep_ref, send_ref, one_ref, mixed_grad_ref, vec_grad_ref, bias_ref,
    two_ref, half_ref, act_ref, inner_ref, *, tile
):
    step = pl.program_id(0)
    rows, width = sum_one_ref.shape
    count = rows // tile
    cut = width // 2

    def rows_of(i):
        return pl.ds(pl.multiple_of(i * tile, tile), tile)

    @pl.when(step == 0)
    def _():
        two_ref[...] = grad_ref[...]
        half_ref[...] = to_half(grad_ref[...])

    bias_ref[...] = jnp.zeros_like(bias_ref)

    def body(i, carry):
        at = rows_of(i)
        act, slope = gelu_parts(u_ref[at, :])
        act_ref[at, :] = to_half(act)
        inner = to_half(mm(half_ref[at, :], r_ref[...]) * slope)
        inner_ref[at, :] = inner
        bias_ref[...] += column_sum(inner)
        two_ref[at, :] += mm_t(inner, e_ref[...])
        return carry

    lax.fori_loop(0, count, body, 0)
    block = u_ref.shape[1]
    steps = pl.num_programs(0)

    def set_grad(at, grad):
        at = pl.ds(pl.multiple_of(at, 128), grad.shape[1])
        keep_ref[:, at] = to_half(grad[:cut])
        send_ref[:, at] = to_half(grad[cut:])

    set_grad(step * block, mm(hidden_t_ref[...], inner_ref[...]))
    set_grad((step + steps) * block, mm(half_t_ref[...], act_ref[...]))

    @pl.when(step == pl.num_programs(0) - 1)
    def _():
        vec_grad_ref[...] = jnp.zeros_like(vec_grad_ref)

        def body(i, carry):
            at = rows_of(i)
            back, gain, shift = norm_back(sum_one_ref[at, :], vec_ref[3:4, :], two_ref[at, :])
            one_ref[at, :] = back
            half = to_half(back)
            half_ref[at, :] = half
            mixed_grad_ref[at, :] = to_half(mm_t(half, out_ref[...]))
            vec_grad_ref[0:1, :] += column_sum(back)
            vec_grad_ref[1:2, :] += gain
            vec_grad_ref[2:3, :] += shift
            return carry

        lax.fori_loop(0, count, body, 0)
        set_grad(2 * steps * block, mm(mixed_t_ref[...], half_ref[...]))


def feed_back(grad, half_t, sum_one, hidden_t, mixed_t, u, enc_mats, enc_ffn, vec):
    rows, width = sum_one.shape
    width_ff = u.shape[1]
    block = 640 if width_ff % 640 == 0 else width_ff
    steps = width_ff // block
    cut = width // 2
    whole = pl.BlockSpec((rows, width), lambda i: (0, 0))
    whole_t = pl.BlockSpec((width, rows), lambda i: (0, 0))
    grads = (cut, 2 * width_ff + width)
    return pl.pallas_call(
        functools.partial(backward_kernel, tile=256),
        grid=(steps,),
        in_specs=[
            whole,
            whole_t,
            whole,
            whole_t,
            whole_t,
            pl.BlockSpec((rows, block), lambda i: (0, i)),
            pl.BlockSpec((width, block), lambda i: (0, i)),
            pl.BlockSpec((width, block), lambda i: (0, i + steps)),
            pl.BlockSpec((width, width), lambda i: (0, 3)),
            pl.BlockSpec(vec.shape, lambda i: (0, 0)),
        ],
        out_specs=[pl.BlockSpec(grads, lambda i: (0, 0))] * 2
        + [
            whole,
            whole,
            pl.BlockSpec((8, width), lambda i: (0, 0)),
            pl.BlockSpec((1, block), lambda i: (0, i)),
        ],
        out_shape=[jax.ShapeDtypeStruct(grads, BF)] * 2
        + [
            jax.ShapeDtypeStruct((rows, width), F32),
            jax.ShapeDtypeStruct((rows, width), BF),
            jax.ShapeDtypeStruct((8, width), F32),
            jax.ShapeDtypeStruct((1, width_ff), F32),
        ],
        scratch_shapes=[
            pltpu.VMEM((rows, width), F32),
            pltpu.VMEM((rows, width), BF),
            pltpu.VMEM((rows, block), BF),
            pltpu.VMEM((rows, block), BF),
        ],
        compiler_params=pltpu.CompilerParams(vmem_limit_bytes=60 * MB),
        cost_estimate=pl.CostEstimate(
            flops=8 * rows * width * width_ff, bytes_accessed=6 * rows * width_ff, transcendentals=rows * width_ff
        ),
        name="feed_back",
    )(grad, half_t, sum_one, hidden_t, mixed_t, u, enc_ffn, enc_ffn, enc_mats, vec)


def attend_back_kernel(
    q_ref, k_ref, v_ref, o_ref, g_ref, log_ref, in_t_ref, x_t_ref, one_ref, wq_ref, wk_ref, wv_ref, *refs, chunk, first
):
    keep_ref, send_ref, grad_ref, vec_ref, kt_ref, dx_ref, dq_ref, dk_ref, dv_ref = refs[-9:]
    step_at = pl.program_id(0)
    width = x_t_ref.shape[0]
    cut = width // 2

    @pl.when(step_at == 0)
    def _():
        dx_ref[...] = one_ref[...]
        if first:
            keep_ref[...] = refs[0][...]
            send_ref[...] = refs[1][...]

    kt_ref[...] = k_ref[...].T
    dk_ref[...] = jnp.zeros_like(dk_ref)
    dv_ref[...] = jnp.zeros_like(dv_ref)

    def step(i, carry):
        at = pl.ds(i * chunk, chunk)
        query = q_ref[at, :] * BF(SCALE)
        grad = g_ref[at, :]
        cross = (grad.astype(F32) * o_ref[at, :].astype(F32)).T
        back = []
        for h in range(2):
            own, own_grad = own_lanes(query, h), own_lanes(grad, h)
            weighted = jnp.sum(cross[h * HDIM : (h + 1) * HDIM], axis=0, keepdims=True)
            probs = jnp.exp(mm_t(k_ref[...], own) - log_ref[0, pl.ds(h, 1), at])
            score_grad = to_half(probs * (mm_t(v_ref[...], own_grad) - weighted))
            dv_ref[...] += mm(to_half(probs), own_grad)
            dk_ref[...] += mm(score_grad, own)
            back.append(mm(kt_ref[...], score_grad))
        dq_ref[at, :] = to_half((join_rows(*back) * SCALE).T)
        return carry

    lax.fori_loop(0, q_ref.shape[0] // chunk, step, 0)
    dq = dq_ref[...]
    dk = to_half(dk_ref[...])
    dv = to_half(dv_ref[...])
    dx_ref[...] += mm_t(dq, wq_ref[...]) + mm_t(dk, wk_ref[...]) + mm_t(dv, wv_ref[...])
    for j, (left_ref, right) in enumerate(((in_t_ref, dq), (in_t_ref, dk), (x_t_ref, dv))):
        wgrad = to_half(mm(left_ref[...], right))
        at = pl.ds(pl.multiple_of(j * width + (first + step_at) * PAIR, PAIR), PAIR)
        keep_ref[:, at] = wgrad[:cut]
        send_ref[:, at] = wgrad[cut:]
    vec_ref[...] = jnp.zeros_like(vec_ref)
    vec_ref[0:1, :] = column_sum(dq)
    vec_ref[1:2, :] = column_sum(dv)

    @pl.when(step_at == pl.num_programs(0) - 1)
    def _():
        grad_ref[...] = dx_ref[...].astype(grad_ref.dtype)


def attend_back(query, keys, values, mixed, grad, log_total, in_t, x_t, so_far, enc_mats, first, count, grads):
    rows, width = query.shape
    pairs = width // PAIR
    cut = width // 2
    own = pl.BlockSpec((rows, PAIR), lambda i: (0, i + first))
    whole = pl.BlockSpec((rows, width), lambda i: (0, 0))
    whole_t = pl.BlockSpec((width, rows), lambda i: (0, 0))
    mats = [pl.BlockSpec((width, PAIR), lambda i, j=j: (0, i + first + j * pairs)) for j in range(3)]
    three = pl.BlockSpec((cut, 3 * width), lambda i: (0, 0))
    return pl.pallas_call(
        functools.partial(attend_back_kernel, chunk=256, first=first),
        grid=(count,),
        in_specs=[own] * 5
        + [pl.BlockSpec((1, 2, rows), lambda i: (i + first, 0, 0)), whole_t, whole_t, whole]
        + mats
        + [three] * len(grads),
        out_specs=[three, three, whole, pl.BlockSpec((8, PAIR), lambda i: (0, i))],
        out_shape=[jax.ShapeDtypeStruct((cut, 3 * width), BF)] * 2
        + [
            jax.ShapeDtypeStruct((rows, width), BF if first + count == pairs else F32),
            jax.ShapeDtypeStruct((8, count * PAIR), F32),
        ],
        scratch_shapes=[
            pltpu.VMEM((PAIR, rows), BF),
            pltpu.VMEM((rows, width), F32),
            pltpu.VMEM((rows, PAIR), BF),
            pltpu.VMEM((rows, PAIR), F32),
            pltpu.VMEM((rows, PAIR), F32),
        ],
        compiler_params=pltpu.CompilerParams(vmem_limit_bytes=60 * MB),
        cost_estimate=pl.CostEstimate(
            flops=10 * rows * rows * width * count, bytes_accessed=16 * rows * width, transcendentals=4 * rows * rows
        ),
        name="attend_back",
    )(query, keys, values, mixed, grad, log_total, in_t, x_t, so_far, enc_mats, enc_mats, enc_mats, *grads)


def heads_forward(query, key_ref, value_ref, prob_ref, spacing=None):
    outs = []
    for pair in range(HEADS // 2):
        lanes = slice(pair * PAIR, (pair + 1) * PAIR)
        keys = key_ref[:, lanes]
        values_t = value_ref[:, lanes].T
        scaled = query[:, lanes] * BF(SCALE)
        mixed = []
        for h in range(2):
            scores = mm_t(keys, own_lanes(scaled, h))
            if spacing is not None:
                row = lax.broadcasted_iota(jnp.int32, scores.shape, 0)
                scores = jnp.where(row % spacing[1] < spacing[0], scores, -jnp.inf)
            weights = jnp.exp(scores - jnp.max(scores, axis=0, keepdims=True))
            probs = weights * (1.0 / jnp.sum(weights, axis=0, keepdims=True))
            prob_ref[2 * pair + h] = probs
            mixed.append(mm(values_t, to_half(probs)))
        outs.append(to_half(join_rows(*mixed).T))
    return jnp.concatenate(outs, axis=1)


def heads_back(query, key_ref, value_ref, prob_ref, grad, dk_ref, dv_ref):
    outs = []
    for pair in range(HEADS // 2):
        lanes = slice(pair * PAIR, (pair + 1) * PAIR)
        keys_t = key_ref[:, lanes].T
        values = value_ref[:, lanes]
        scaled = query[:, lanes] * BF(SCALE)
        dk = dv = None
        back = []
        for h in range(2):
            own, own_grad = own_lanes(scaled, h), own_lanes(grad[:, lanes], h)
            probs = prob_ref[2 * pair + h]
            prob_grad = mm_t(values, own_grad)
            weighted = jnp.sum(probs * prob_grad, axis=0, keepdims=True)
            score_grad = to_half(probs * (prob_grad - weighted))
            back.append(mm(keys_t, score_grad))
            k_part, v_part = mm(score_grad, own), mm(to_half(probs), own_grad)
            dk = k_part if h == 0 else dk + k_part
            dv = v_part if h == 0 else dv + v_part
        dk_ref[:, lanes] = to_half(dk)
        dv_ref[:, lanes] = to_half(dv)
        outs.append(to_half((join_rows(*back) * SCALE).T))
    return jnp.concatenate(outs, axis=1)


def decode_kernel(
    x_ref, query_ref, target_ref, valid_ref, w_ref, f_ref, head_ref, vec_ref, bias_ref, mem_ref, pos_ref, turn_ref,
    w_keep_ref, w_send_ref, f_keep_ref, f_send_ref, in_grad_ref, query_grad_ref, mem_grad_ref, vec_grad_ref, head_grad_ref, bias_grad_ref,
    mem_in, mem_half, cross_k, cross_v, cross_dk, cross_dv, cross_p,
    self_k, self_v, self_dk, self_dv, self_p, u_ref, act_ref, acc_ref, left_ref, *, spacing, joints, block
):
    width = x_ref.shape[1]
    width_ff = u_ref.shape[1]
    blocks = width_ff // block

    def mat(i):
        return w_ref[:, i * width : (i + 1) * width]

    cut = width // 2

    def left_of(values):
        return turned(turn_ref[...], values)

    def set_mat(i, left_t, right):
        grad = to_half(mm(left_t, right))
        w_keep_ref[:, i * width : (i + 1) * width] = grad[:cut]
        w_send_ref[:, i * width : (i + 1) * width] = grad[cut:]

    def set_ffn(at, left_t, right):
        grad = to_half(mm(left_t, right))
        f_keep_ref[:, at] = grad[:cut]
        f_send_ref[:, at] = grad[cut:]

    def vec(i):
        return vec_ref[i : i + 1, :]

    def set_vec(i, value):
        vec_grad_ref[i - 8 : i - 7, :] = value

    def lanes(i, start=0):
        return pl.ds(pl.multiple_of(start + i * block, 128), block)

    vec_grad_ref[...] = jnp.zeros_like(vec_grad_ref)
    x = x_ref[...]
    x_float = x.astype(F32)
    places = query_ref[...]
    self_in = to_half(x_float + places)
    self_q = to_half(mm(self_in, mat(0)) + vec(8))
    self_k[...] = to_half(mm(self_in, mat(1)))
    self_v[...] = to_half(mm(x, mat(2)) + vec(9))
    self_mixed = heads_forward(self_q, self_k, self_v, self_p, spacing)
    sum_one = x_float + mm(self_mixed, mat(3)) + vec(10)
    one = layer_norm(sum_one, vec(11), vec(12))
    cross_in = to_half(one + places)
    cross_q = to_half(mm(cross_in, mat(4)) + vec(13))
    mem_in[...] = to_half(mem_ref[...] + pos_ref[...])
    mem_half[...] = to_half(mem_ref[...])
    cross_k[...] = to_half(mm(mem_in[...], mat(5)))
    cross_v[...] = to_half(mm(mem_half[...], mat(6)) + vec(14))
    cross_mixed = heads_forward(cross_q, cross_k, cross_v, cross_p)
    sum_two = one + mm(cross_mixed, mat(7)) + vec(15)
    two = layer_norm(sum_two, vec(16), vec(17))
    two_half = to_half(two)
    acc_ref[...] = two + vec(18)

    def forward(i, carry):
        u = mm(two_half, f_ref[:, lanes(i)]) + bias_ref[:, lanes(i)]
        u_ref[:, lanes(i)] = u
        acc_ref[...] += mm_t(to_half(gelu(u)), f_ref[:, lanes(i, width_ff)])
        return carry

    lax.fori_loop(0, blocks, forward, 0)
    sum_three = acc_ref[...]
    three_half = to_half(layer_norm(sum_three, vec(19), vec(20)))
    error = mm_t(three_half, head_ref[...]) - target_ref[...]
    pred_grad = to_half(error * lax.rsqrt(error * error + 1.0) * valid_ref[...] / joints)
    head_grad_ref[...] = mm(pred_grad.T, three_half)
    sum_three_grad, gain, shift = norm_back(sum_three, vec(19), mm(pred_grad, head_ref[...]))
    set_vec(18, column_sum(sum_three_grad))
    set_vec(19, gain)
    set_vec(20, shift)
    out_grad = to_half(sum_three_grad)
    left_ref[0] = left_of(out_grad)
    left_ref[1] = left_of(two_half)
    acc_ref[...] = sum_three_grad

    def backward(i, carry):
        act, slope = gelu_parts(u_ref[:, lanes(i)])
        inner = to_half(mm(out_grad, f_ref[:, lanes(i, width_ff)]) * slope)
        bias_grad_ref[:, lanes(i)] = column_sum(inner)
        acc_ref[...] += mm_t(inner, f_ref[:, lanes(i)])
        set_ffn(lanes(i), left_ref[1], inner)
        set_ffn(lanes(i, width_ff), left_ref[0], to_half(act))
        return carry

    lax.fori_loop(0, blocks, backward, 0)
    sum_two_grad, gain, shift = norm_back(sum_two, vec(16), acc_ref[...])
    set_vec(15, column_sum(sum_two_grad))
    set_vec(16, gain)
    set_vec(17, shift)
    out_grad = to_half(sum_two_grad)
    set_mat(7, left_of(cross_mixed), out_grad)
    mixed_grad = to_half(mm_t(out_grad, mat(7)))
    cross_dq = heads_back(cross_q, cross_k, cross_v, cross_p, mixed_grad, cross_dk, cross_dv)
    set_vec(13, column_sum(cross_dq))
    set_vec(14, column_sum(cross_dv[...]))
    mem_grad_ref[...] = mm_t(cross_dk[...], mat(5)) + mm_t(cross_dv[...], mat(6))
    set_mat(4, left_of(cross_in), cross_dq)
    set_mat(5, left_of(mem_in[...]), cross_dk[...])
    set_mat(6, left_of(mem_half[...]), cross_dv[...])
    cross_in_grad = mm_t(cross_dq, mat(4))
    sum_one_grad, gain, shift = norm_back(sum_one, vec(11), sum_two_grad + cross_in_grad)
    set_vec(10, column_sum(sum_one_grad))
    set_vec(11, gain)
    set_vec(12, shift)
    out_grad = to_half(sum_one_grad)
    set_mat(3, left_of(self_mixed), out_grad)
    mixed_grad = to_half(mm_t(out_grad, mat(3)))
    self_dq = heads_back(self_q, self_k, self_v, self_p, mixed_grad, self_dk, self_dv)
    set_vec(8, column_sum(self_dq))
    set_vec(9, column_sum(self_dv[...]))
    in_t = left_of(self_in)
    set_mat(0, in_t, self_dq)
    set_mat(1, in_t, self_dk[...])
    set_mat(2, left_of(x), self_dv[...])
    self_in_grad = mm_t(self_dq, mat(0)) + mm_t(self_dk[...], mat(1))
    in_grad_ref[...] = to_half(sum_one_grad + self_in_grad + mm_t(self_dv[...], mat(2)))
    query_grad_ref[...] = self_in_grad + cross_in_grad


def decode(x, places, target, valid, weights, ffn, head_t, vec, bias, memory, positions, turn, spacing, joints):
    rows, width = x.shape
    mem_rows = memory.shape[0]
    width_ff = bias.shape[1]
    half = lambda n: pltpu.VMEM((n, width), BF)
    return pl.pallas_call(
        functools.partial(
            decode_kernel, spacing=spacing, joints=joints, block=640 if width_ff % 640 == 0 else width_ff
        ),
        out_shape=[
            jax.ShapeDtypeStruct((width // 2, 8 * width), BF),
            jax.ShapeDtypeStruct((width // 2, 8 * width), BF),
            jax.ShapeDtypeStruct((width // 2, 2 * width_ff), BF),
            jax.ShapeDtypeStruct((width // 2, 2 * width_ff), BF),
            jax.ShapeDtypeStruct((rows, width), BF),
            jax.ShapeDtypeStruct((rows, width), F32),
            jax.ShapeDtypeStruct((mem_rows, width), F32),
            jax.ShapeDtypeStruct((16, width), F32),
            jax.ShapeDtypeStruct(head_t.shape, F32),
            jax.ShapeDtypeStruct((1, width_ff), F32),
        ],
        scratch_shapes=[half(mem_rows)] * 6
        + [pltpu.VMEM((HEADS, mem_rows, rows), F32)]
        + [half(rows)] * 4
        + [
            pltpu.VMEM((HEADS, rows, rows), F32),
            pltpu.VMEM((rows, width_ff), F32),
            pltpu.VMEM((rows, width_ff), BF),
            pltpu.VMEM((rows, width), F32),
            pltpu.VMEM((2, width, rows), BF),
        ],
        compiler_params=pltpu.CompilerParams(vmem_limit_bytes=60 * MB),
        cost_estimate=pl.CostEstimate(
            flops=12 * mem_rows * width * width, bytes_accessed=4 * weights.size, transcendentals=rows * width_ff
        ),
        name="decode",
    )(x, places, target, valid, weights, ffn, head_t, vec, bias, memory, positions, turn)


def adamw(weight, gradient, moment_one, moment_two, step_rate):
    moment_one = beta_first * moment_one + (1.0 - beta_first) * gradient
    moment_two = beta_second * moment_two + (1.0 - beta_second) * gradient * gradient
    mean_hat = moment_one / (1.0 - beta_first**STEP)
    square_hat = moment_two / (1.0 - beta_second**STEP)
    updated = weight - step_rate * (
        mean_hat / (jnp.sqrt(square_hat) + epsilon) + decay_rate * weight
    )
    return (moment_one, moment_two, updated, updated.astype(BF))


def update_kernel(*refs, rates):
    count = len(rates)
    ins, outs = refs[: 4 * count], refs[4 * count :]
    for i, rate in enumerate(rates):
        values = adamw(*(ref[...] for ref in ins[4 * i : 4 * i + 4]), rate)
        for ref, value in zip(outs[4 * i : 4 * i + 4], values):
            ref[...] = value


def update(groups, rates):
    shapes = []
    for group in groups:
        shapes += [jax.ShapeDtypeStruct(group[0].shape, F32)] * 3
        shapes.append(jax.ShapeDtypeStruct(group[0].shape, BF))
    outs = pl.pallas_call(
        functools.partial(update_kernel, rates=rates),
        out_shape=shapes,
        compiler_params=pltpu.CompilerParams(vmem_limit_bytes=56 * MB),
        name="update",
    )(*(array for group in groups for array in group))
    return [outs[4 * i : 4 * i + 4] for i in range(len(groups))]


def pad_to(values, rows, columns):
    return jnp.pad(values, ((0, rows - values.shape[0]), (0, columns - values.shape[1])))


def side_by_side(mats):
    return jnp.concatenate([mats[i] for i in range(mats.shape[0])], axis=1)


def gather(columns):
    return lax.all_gather(columns, ALL, axis=0, tiled=True)


def width_bits(axis):
    return (lax.axis_size(axis) - 1).bit_length()


def bit_groups(one_by_one=False):
    low = width_bits("seq")
    others = list(range(low + width_bits("dp") - 1, low, -1))
    groups = [[low]]
    for bits, most in ((others, 2), (list(range(low)), 1 if one_by_one else 2)):
        groups += [bits[i : i + most] for i in range(0, len(bits), most)]
    return groups


def spread(bits, place):
    return sum(((place >> k) & 1) << bit for k, bit in enumerate(reversed(bits)))


def turn_matrices(width):
    order = [bit for bits in bit_groups() for bit in bits]
    devices = 1 << len(order)
    relative = np.array([spread(order, j) for j in range(devices)], np.int32)
    shard = width // devices
    source = jnp.bitwise_xor(jnp.asarray(relative), lax.axis_index(ALL).astype(jnp.int32))
    source = (source[:, None] * shard + jnp.arange(shard, dtype=jnp.int32)[None, :]).reshape(width)
    places = jnp.arange(width, dtype=jnp.int32)
    return (source[:, None] == places[None, :]).astype(BF), (source[None, :] == places[:, None]).astype(BF)


def exchange(values, distance):
    low = width_bits("seq")
    axis, distance = ("dp", distance >> low) if distance >> low else ("seq", distance)
    pairs = [(i, i ^ distance) for i in range(lax.axis_size(axis))]
    return lax.ppermute(values, axis, pairs)


class Sum:
    def __init__(self, blocks, one_by_one=False):
        self.blocks = list(blocks)
        self.groups = bit_groups(one_by_one)
        self.arrived = None

    def start(self):
        bits = self.groups.pop(0)
        self.arrived = [exchange(block, spread(bits, j)) for j, block in enumerate(self.blocks) if j]

    def add(self):
        arrays = [self.blocks[0]] + self.arrived
        count = 1 << len(self.groups[0]) if self.groups else 1
        rows = arrays[0].shape[-2] // count
        totals = []
        for j in range(count):
            parts = [array[..., j * rows : (j + 1) * rows, :].astype(F32) for array in arrays]
            total = functools.reduce(jnp.add, parts)
            totals.append(to_half(total) if self.groups else total)
        self.blocks = totals
        self.arrived = None

    def step(self):
        self.add()
        if self.groups:
            self.start()

    def finish(self):
        while self.groups or self.arrived is not None:
            if self.arrived is None:
                self.start()
            self.step()
        return self.blocks[0]


class Gather:
    def __init__(self, value):
        self.value = value
        self.groups = bit_groups()
        self.arrived = None

    def start(self):
        bits = self.groups.pop()
        self.arrived = [exchange(self.value, spread(bits, j)) for j in range(1, 1 << len(bits))]

    def step(self):
        if not self.groups:
            return self.value, self.arrived[0]
        self.value = jnp.concatenate([self.value] + self.arrived)
        self.start()

    def up_to_last(self):
        while len(self.groups) > 1:
            self.step()

    def finish(self):
        halves = self.step()
        while halves is None:
            halves = self.step()
        return halves


def swap(pieces):
    return lax.all_to_all(pieces, "seq", 0, 0, tiled=True)


def tie(values, *sums):
    values, arrived = lax.optimization_barrier((values, [s.arrived for s in sums]))
    for s, a in zip(sums, arrived):
        s.arrived = a
    return values


def per_device(
    enc_input,
    dec_input,
    targets,
    lengths,
    attention_mats,
    expand_mats,
    reduce_mats,
    action_head,
    query_pos,
    vectors,
    expand_bias,
    *moments,
):
    ranks = lax.axis_size("seq")
    seq_index = lax.axis_index("seq")
    items, enc_part, width = enc_input.shape
    dec_part = dec_input.shape[1]
    joints = targets.shape[2]
    width_ff = expand_mats.shape[2]
    shard = attention_mats.shape[1]
    bias_part = expand_bias.shape[0]
    n_query, n_vec = query_pos.shape[0], vectors.shape[0]
    vec_at = (n_query + 7) // 8 * 8
    head_at = (vec_at + n_vec + 7) // 8 * 8
    n_small = (head_at + joints + 127) // 128 * 128
    devices = width // shard
    dec_block = (dec_part + 15) // 16 * 16
    dec_rows = ranks * dec_block

    reduce_t = jnp.swapaxes(reduce_mats, 1, 2)
    half_mats = to_half(attention_mats)
    half_expand = to_half(expand_mats)
    half_reduce = to_half(reduce_t)
    small_local = to_half(
        jnp.concatenate(
            [
                pad_to(query_pos.T, shard, vec_at),
                pad_to(vectors.T, shard, head_at - vec_at),
                pad_to(action_head, shard, n_small - head_at),
            ],
            axis=1,
        )
    )
    bias_local = to_half(jnp.pad(expand_bias, (0, shard * 128 - bias_part)).reshape(shard, 128))
    att_all = Gather(jnp.concatenate([side_by_side(half_mats[0:4]), small_local, bias_local], axis=1))
    ffn_all = Gather(jnp.concatenate([half_expand[1], half_reduce[1]], axis=1))
    att_all.start()
    enc_ffn = gather(jnp.concatenate([half_expand[0], half_reduce[0]], axis=1))
    dec_mats = gather(side_by_side(half_mats[4:12]))

    assert items == ranks
    def spaced(values):
        parts = values.reshape(ranks, dec_part, values.shape[-1])
        return jnp.pad(parts, ((0, 0), (0, dec_block - dec_part), (0, 0)))

    rows_in = swap(jnp.concatenate([enc_input, spaced(dec_input)], axis=1))
    enc_x = rows_in[:, :enc_part].reshape(ranks * enc_part, width)
    dec_x = rows_in[:, enc_part:].reshape(dec_rows, width)
    target = swap(jnp.pad(spaced(targets), ((0, 0), (0, 0), (0, 128 - joints)))).reshape(dec_rows, 128)
    turn, turn_back = turn_matrices(width)
    positions = jnp.asarray(sine_table(ranks * enc_part, width))
    att_all.up_to_last()
    ffn_all.value = tie(ffn_all.value, att_all)
    enc_att = settle(*att_all.finish(), turn_back, 4 * width + n_small + 128)
    ffn_all.start()
    length = lengths[seq_index]
    row = jnp.arange(dec_rows)
    place = row % dec_block
    valid = (place < dec_part) & (row // dec_block * dec_part + place < length)
    valid = jnp.broadcast_to(valid.astype(F32)[:, None], (dec_rows, 128))

    at = 4 * width
    small = enc_att[:, at : at + n_small].T
    bias_all = enc_att[:, at + n_small :].reshape(devices, shard * 128)
    bias_all = bias_all[:, :bias_part].reshape(1, 2 * width_ff).astype(F32)
    query_whole = spaced(small[:n_query].astype(F32)).reshape(dec_rows, width)
    vec = pad_to(small[vec_at : vec_at + n_vec].astype(F32), (n_vec + 7) // 8 * 8, width)
    head_t = pad_to(small[head_at : head_at + joints], 128, width)
    query, keys, values, mixed, log_total = attend(enc_x, positions, enc_att, vec)
    block = 640 if width_ff % 640 == 0 else width_ff
    query, keys, values, mixed, log_total, target, valid, query_whole, head_t, dec_x = tie(
        (query, keys, values, mixed, log_total, target, valid, query_whole, head_t, dec_x), ffn_all
    )
    ffn_all.step()
    sum_one, hidden, u, sum_two, memory = tie(
        feed_forward(mixed, enc_x, enc_att, vec, enc_ffn, bias_all[:, :width_ff]), ffn_all
    )
    ffn_all.up_to_last()
    memory, in_t, x_t, mixed_t, hidden_t = tie((memory, *lefts(enc_x, positions, mixed, hidden, turn)), ffn_all)
    dec_ffn = settle(*ffn_all.finish(), turn_back, block)
    (
        w_keep, w_send, f_keep, f_send,
        dec_in_grad, query_grad, memory_grad, dec_vec_grads, head_grad_t, dec_bias_grad,
    ) = decode(
        dec_x, query_whole, target, valid, dec_mats, dec_ffn, head_t, vec, bias_all[:, width_ff:], memory, positions, turn,
        (dec_part, dec_block), joints,
    )
    dec_f, dec_att = Sum([f_keep, f_send], True), Sum([w_keep, w_send], True)
    dec_f.start()
    dec_att.start()
    two_grad, half_t, vec_grads_c = tie(last_norm_back(memory_grad, sum_two, vec, turn), dec_f, dec_att)
    dec_f.step()
    keep, send, one_grad, mixed_grad, vec_grads_b, enc_bias_grad, att_held = tie(
        [
            *feed_back(two_grad, half_t, sum_one, hidden_t, mixed_t, u, enc_att, enc_ffn, vec),
            (dec_att.blocks, dec_att.arrived),
        ],
        dec_f,
    )
    dec_att.blocks, dec_att.arrived = att_held
    enc_ffn_sum = Sum([keep, send], True)
    enc_ffn_sum.start()
    dec_f.step()
    dec_att.step()

    def back(so_far, first, count, grads):
        return attend_back(
            query, keys, values, mixed, mixed_grad, log_total, in_t, x_t, so_far, enc_att, first, count, grads
        )

    pairs = HEADS // 2
    keep, send, so_far, vec_grads_d = tie(back(one_grad, 0, 1, ()), enc_ffn_sum)
    enc_ffn_sum.add()
    so_far, enc_ffn_sum.blocks = tie((so_far, enc_ffn_sum.blocks), dec_f, dec_att)
    enc_ffn_sum.start()
    dec_f.step()
    dec_att.step()
    keep, send, so_far, vec_grads_e = tie(back(so_far, 1, pairs - 2, (keep, send)), dec_f, dec_att)
    dec_ffn_total = dec_f.finish()
    dec_att.step()
    dec_grad = swap(dec_in_grad.reshape(ranks, dec_block, width))[:, :dec_part]
    vec_grads = jnp.concatenate([vec_grads_b[:3], vec_grads_c[:3], dec_vec_grads[: n_vec - 8]])
    small_rows = jnp.concatenate(
        [
            pad_to(query_grad.reshape(ranks, dec_block, width)[:, :dec_part].reshape(n_query, width), vec_at + 2, width),
            pad_to(vec_grads, head_at - vec_at - 2, width),
            pad_to(head_grad_t[:joints], n_small - head_at, width),
        ]
    )
    bias_grad = jnp.concatenate([enc_bias_grad, dec_bias_grad], axis=1).reshape(devices, bias_part)
    bias_grad = pad_to(bias_grad, devices, shard * 128).reshape(width, 128)
    small_grad = to_half(
        jnp.concatenate([mm_t(turn, to_half(small_rows)), mm(turn, to_half(bias_grad))], axis=1)
    )
    keep, send, enc_grad, vec_grads_f, small_grad, dec_grad = tie(
        [*back(so_far, pairs - 1, 1, (keep, send)), small_grad, dec_grad], dec_att, enc_ffn_sum
    )
    dec_att_total = dec_att.finish()
    enc_grad = swap(enc_grad.reshape(ranks, enc_part, width))
    enc_ffn_sum.step()
    late_rows = jnp.concatenate([vec_grads_d[:2], vec_grads_e[:2], vec_grads_f[:2]], axis=1)
    late_grad = to_half(mm_t(turn, to_half(pad_to(late_rows, 128, width))))
    half = width // 2
    last = Sum(
        [
            jnp.concatenate([keep, small_grad[:half], late_grad[:half]], axis=1),
            jnp.concatenate([send, small_grad[half:], late_grad[half:]], axis=1),
        ]
    )
    last.start()
    dec_att_total = tie(dec_att_total, last)
    last.step()
    dec_ffn_total = tie(dec_ffn_total, enc_ffn_sum)
    enc_ffn_sum.step()
    dec_ffn_total, enc_grad = tie((dec_ffn_total, enc_grad), last, enc_ffn_sum)
    enc_ffn_total, last_total = enc_ffn_sum.finish(), last.finish()
    outputs = [enc_grad, dec_grad]

    small_total = last_total[:, 3 * width :]
    gradients = (
        jnp.stack(
            [last_total[:, i * width : (i + 1) * width] for i in range(3)]
            + [enc_ffn_total[:, 2 * width_ff :]]
            + [dec_att_total[:, i * width : (i + 1) * width] for i in range(8)]
        ),
        jnp.stack([enc_ffn_total[:, :width_ff], dec_ffn_total[:, :width_ff]]),
        jnp.stack([enc_ffn_total[:, width_ff : 2 * width_ff], dec_ffn_total[:, width_ff:]]),
        small_total[:, head_at : head_at + joints],
        small_total[:, :n_query],
        jnp.concatenate(
            [small_total[:, n_small + 128 : n_small + 130], small_total[:, vec_at + 2 : vec_at + n_vec]], axis=1
        ),
        small_total[:, n_small : n_small + 128].reshape(1, -1)[:, :bias_part],
    )

    def views(mats, expand, reduce, head, query, vector, bias):
        return (mats, expand, jnp.swapaxes(reduce, 1, 2), head, query.T, vector.T, bias.reshape(1, -1))

    weights = views(attention_mats, expand_mats, reduce_mats, action_head, query_pos, vectors, expand_bias)
    firsts, seconds = views(*moments[:7]), views(*moments[7:])
    rates = (rate_matrix,) * 4 + (rate_vector,) * 3
    for i, results in enumerate(update(list(zip(weights, gradients, firsts, seconds)), rates)):
        if i == 2:
            results = [jnp.swapaxes(value, 1, 2) for value in results]
        if i in (4, 5):
            results = [value.T for value in results]
        if i == 6:
            results = [value.reshape(-1) for value in results]
        outputs.extend(results)
    return tuple(outputs)


def solution(mesh):
    rows = P("dp", "seq", None)
    weight_specs = (
        P(None, ALL, None),
        P(None, ALL, None),
        P(None, None, ALL),
        P(ALL, None),
        P(None, ALL),
        P(None, ALL),
        P(ALL),
    )
    in_specs = (rows, rows, rows, P("dp")) + weight_specs * 3
    out_specs = (rows, rows) + tuple(spec for spec in weight_specs for unused in range(4))
    return jax.shard_map(
        per_device, mesh=mesh, in_specs=in_specs, out_specs=out_specs, check_vma=False
    )
```

profile of v0, /device:TPU:0, one launch (start us, length us, event | category | flops | bytes accessed | tf_op | source)
XLA Modules:
  0.0 435.8 jit_solution(15990335612464102850)
XLA Ops:
  10.5 5.0 %collective-permute-start.2 = (bf16[16,2432]{1,0:T(8,128)(2,1)S(1)}, bf16[16,2432]{1,0:T(8,128)(2,1)S(1)}, u32[]{:S(2)}, u32[]{:S(2)}) collective-permute-start(bf16[16,2432]{1,0:T(8,128)(2,1)S(1)} %concatenate.62), channel_id=1, source_target_pairs={{0,3},{1,2},{2,1},{3,0},{4,7},{5,6},{6,5},{7,4},{8,11},{9,10},{10,... | collective-permute-start | bytes 233480 | tf_op jit(solution)/shard_map/ppermute | solution.py:798
  17.4 5.1 %all-to-all-start = ((bf16[4,288,512]{2,1,0:T(8,128)(2,1)}), bf16[4,288,512]{2,1,0:T(8,128)(2,1)}, u32[]{:S(2)}, u32[]{:S(2)}) async-start(bf16[4,288,512]{2,1,0:T(8,128)(2,1)} %fusion.1), calls=%async_computation | async-start | bytes 2359296 | tf_op jit(solution)/shard_map/all_to_all | solution.py:864
  24.2 2.5 collective-permute-start.5
  27.8 7.7 %collective-permute-done.5 = bf16[64,2432]{1,0:T(8,128)(2,1)S(1)} collective-permute-done((bf16[64,2432]{1,0:T(8,128)(2,1)S(1)}, bf16[64,2432]{1,0:T(8,128)(2,1)S(1)}, u32[]{:S(2)}, u32[]{:S(2)}) %collective-permute-start.5) | collective-permute-done | bytes 311328 | tf_op jit(solution)/shard_map/ppermute | solution.py:798
  35.4 5.2 %collective-permute-done.4 = bf16[64,2432]{1,0:T(8,128)(2,1)S(1)} collective-permute-done((bf16[64,2432]{1,0:T(8,128)(2,1)S(1)}, bf16[64,2432]{1,0:T(8,128)(2,1)S(1)}, u32[]{:S(2)}, u32[]{:S(2)}) %collective-permute-start.4) | collective-permute-done | bytes 311328 | tf_op jit(solution)/shard_map/ppermute | solution.py:798
  43.9 3.5 collective-permute-start.9
  72.4 4.9 %all-to-all-start.1 = ((f32[4,32,128]{2,1,0:T(8,128)}), f32[4,32,128]{2,1,0:T(8,128)}, u32[]{:S(2)}, u32[]{:S(2)}) async-start(f32[4,32,128]{2,1,0:T(8,128)} %pad.123), calls=%async_computation.1 | async-start | bytes 131072 | tf_op jit(solution)/shard_map/all_to_all | solution.py:864
  79.6 33.3 %attend.1 = (bf16[1024,512]{1,0:T(8,128)(2,1)}, bf16[1024,512]{1,0:T(8,128)(2,1)}, bf16[1024,512]{1,0:T(8,128)(2,1)}, bf16[1024,512]{1,0:T(8,128)(2,1)}, f32[4,2,1024]{2,1,0:T(2,128)}) custom-call(bf16[1024,512]{1,0:T(8,128)(2,1)} %bitcast.135, f32[1024,512]{1,0:T(8,128)} %constant.59.clone.pos_ref, bf16[512,2432]{1,0:T(8,128)(2,1)} %copy-done.4, ...), custom_call_target="tpu_custom_call" | custom-call | flops 8589934592 | bytes 6291456 | tf_op jit(solution)/shard_map/attend/pallas_call | solution.py:157
  124.5 23.2 %feed_forward.1 = (f32[1024,512]{1,0:T(8,128)}, bf16[1024,512]{1,0:T(8,128)(2,1)}, f32[1024,3200]{1,0:T(8,128)}, f32[1024,512]{1,0:T(8,128)}, f32[1024,512]{1,0:T(8,128)}) custom-call(bf16[1024,512]{1,0:T(8,128)(2,1)} %get-tuple-element.208.mixed_ref.o_ref, bf16[1024,512]{1,0:T(8,128)(2,1)} %bitcast.136, bf16[512,2432]{1,0:T(8,128)(2,1)} %copy-done.4, ...), custom_call_target="tpu_custom_call" | custom-call | flops 6710886400 | bytes 13107200 | tf_op jit(solution)/shard_map/feed_forward/pallas_call | solution.py:221
  147.7 14.7 %collective-permute-done.11 = bf16[64,6400]{1,0:T(8,128)(2,1)S(1)} collective-permute-done((bf16[64,6400]{1,0:T(8,128)(2,1)}, bf16[64,6400]{1,0:T(8,128)(2,1)S(1)}, u32[]{:S(2)}, u32[]{:S(2)}) %collective-permute-start.11) | collective-permute-done | bytes 819232 | tf_op jit(solution)/shard_map/ppermute | solution.py:798
  162.4 4.5 %collective-permute-done.10 = bf16[64,6400]{1,0:T(8,128)(2,1)S(1)} collective-permute-done((bf16[64,6400]{1,0:T(8,128)(2,1)}, bf16[64,6400]{1,0:T(8,128)(2,1)S(1)}, u32[]{:S(2)}, u32[]{:S(2)}) %collective-permute-start.10) | collective-permute-done | bytes 819232 | tf_op jit(solution)/shard_map/ppermute | solution.py:798
  168.2 2.4 lefts.1
  172.6 5.8 %collective-permute-done.13.bottom_ref = bf16[256,6400]{1,0:T(8,128)(2,1)S(1)} collective-permute-done((bf16[256,6400]{1,0:T(8,128)(2,1)S(1)}, bf16[256,6400]{1,0:T(8,128)(2,1)S(1)}, u32[]{:S(2)}, u32[]{:S(2)}) %collective-permute-start.13) | collective-permute-done | bytes 3276832 | tf_op jit(solution)/shard_map/ppermute | solution.py:798
  178.5 6.9 %settle.3.f_ref = bf16[512,6400]{1,0:T(8,128)(2,1)S(1)} custom-call(bf16[256,6400]{1,0:T(8,128)(2,1)S(1)} %constant_dynamic-update-slice_fusion.19.top_ref, bf16[256,6400]{1,0:T(8,128)(2,1)S(1)} %collective-permute-done.13.bottom_ref, bf16[512,512]{1,0:T(8,128)(2,1)S(1)} %get-tuple-element.436.turn_ref), custom_call_target="tpu_custom_call" | custom-call | flops 3355443200 | bytes 13107200 | tf_op jit(solution)/shard_map/settle/pallas_call | solution.py:108
  185.3 2.8 copy-done
  188.1 34.9 %decode.1 = (bf16[256,4096]{1,0:T(8,128)(2,1)}, bf16[256,4096]{1,0:T(8,128)(2,1)}, bf16[256,6400]{1,0:T(8,128)(2,1)}, bf16[256,6400]{1,0:T(8,128)(2,1)}, bf16[12...) custom-call(bf16[128,512]{1,0:T(8,128)(2,1)} %bitcast.143, ...), custom_call_target="tpu_custom_call" | custom-call | flops 3221225472 | bytes 8388608 | tf_op jit(solution)/shard_map/decode/pallas_call | solution.py:686
  223.6 5.3 %all-to-all-start.2 = ((bf16[4,32,512]{2,1,0:T(8,128)(2,1)}), bf16[4,32,512]{2,1,0:T(8,128)(2,1)}, u32[]{:S(2)}, u32[]{:S(2)}) async-start(bf16[4,32,512]{2,1,0:T(8,128)(2,1)} %bitcast.147), calls=%async_computation.2 | async-start | bytes 262144 | tf_op jit(solution)/shard_map/all_to_all | solution.py:864
  235.7 3.6 add_convert_fusion.7
  242.9 37.2 %feed_back.1 = (bf16[256,6912]{1,0:T(8,128)(2,1)}, bf16[256,6912]{1,0:T(8,128)(2,1)}, f32[1024,512]{1,0:T(8,128)}, bf16[1024,512]{1,0:T(8,128)(2,1)}, f32[8,512]{1,0:T(8,128)}, /*index=5*/f32[1,3200]{1,0:T(1,128)}) custom-call(f32[1024,512]{1,0:T(8,128)} %copy-done.14, bf16[512,1024]{1,0:T(8,128)(2,1)} %copy-done.15, ...), custom_call_target="tpu_custom_call" | custom-call | flops 13421772800 | bytes 19660800 | tf_op jit(solution)/shard_map/feed_back/pallas_call | solution.py:375
  281.9 3.0 add_convert_fusion.15
  287.0 3.1 add_convert_fusion.8
  295.1 12.9 %attend_back.3 = (bf16[256,1536]{1,0:T(8,128)(2,1)}, bf16[256,1536]{1,0:T(8,128)(2,1)}, f32[1024,512]{1,0:T(8,128)}, f32[8,128]{1,0:T(8,128)}) custom-call(bf16[1024,512]{1,0:T(8,128)(2,1)} %get-tuple-element.254.q_ref, bf16[1024,512]{1,0:T(8,128)(2,1)} %get-tuple-element.255.k_ref, bf16[1024,512]{1,0:T(8,128)(2,1)} %get-tuple-element.256.v_ref, ...), custom_call_target="tpu_custom_call" | custom-call | flops 5368709120 | bytes 8388608 | tf_op jit(solution)/shard_map/attend_back/pallas_call | solution.py:482
  308.1 4.4 %add_convert_fusion = (bf16[64,6912]{1,0:T(8,128)(2,1)}, bf16[64,6912]{1,0:T(8,128)(2,1)}, bf16[64,6912]{1,0:T(8,128)(2,1)}, bf16[64,6912]{1,0:T(8,128)(2,1)}) fusion(bf16[256,6912]{1,0:T(8,128)(2,1)} %collective-permute-done.19, bf16[256,6912]{1,0:T(8,128)(2,1)S(1)} %copy-done.22), kind=kLoop, calls=%fused_computation.2 | loop fusion | flops 7077888 | bytes 10616832 | tf_op jit(solution)/shard_map/convert_element_type | solution.py:32
  312.5 3.9 collective-permute-done.22
  317.5 2.4 collective-permute-start.24
  325.7 21.3 %attend_back.4 = (bf16[256,1536]{1,0:T(8,128)(2,1)}, bf16[256,1536]{1,0:T(8,128)(2,1)}, f32[1024,512]{1,0:T(8,128)}, f32[8,256]{1,0:T(8,128)}) custom-call(bf16[1024,512]{1,0:T(8,128)(2,1)} %get-tuple-element.254.q_ref, bf16[1024,512]{1,0:T(8,128)(2,1)} %get-tuple-element.255.k_ref, bf16[1024,512]{1,0:T(8,128)(2,1)} %get-tuple-element.256.v_ref, ...), custom_call_target="tpu_custom_call" | custom-call | flops 10737418240 | bytes 8388608 | tf_op jit(solution)/shard_map/attend_back/pallas_call | solution.py:482
  348.5 12.7 %attend_back.5 = (bf16[256,1536]{1,0:T(8,128)(2,1)}, bf16[256,1536]{1,0:T(8,128)(2,1)}, bf16[1024,512]{1,0:T(8,128)(2,1)}, f32[8,128]{1,0:T(8,128)}) custom-call(bf16[1024,512]{1,0:T(8,128)(2,1)} %get-tuple-element.254.q_ref, bf16[1024,512]{1,0:T(8,128)(2,1)} %get-tuple-element.255.k_ref, bf16[1024,512]{1,0:T(8,128)(2,1)} %get-tuple-element.256.v_ref, ...), custom_call_target="tpu_custom_call" | custom-call | flops 5368709120 | bytes 8388608 | tf_op jit(solution)/shard_map/attend_back/pallas_call | solution.py:482
  364.4 2.7 add_convert_fusion.12
  369.9 3.8 all-to-all-start.3
  375.1 4.1 collective-permute-done.30
  387.2 22.6 %collective-permute-done.35 = bf16[16,6912]{1,0:T(8,128)(2,1)S(1)} collective-permute-done((bf16[16,6912]{1,0:T(8,128)(2,1)S(1)}, bf16[16,6912]{1,0:T(8,128)(2,1)S(1)}, u32[]{:S(2)}, u32[]{:S(2)}) %collective-permute-start.35) | collective-permute-done | bytes 221216 | tf_op jit(solution)/shard_map/ppermute | solution.py:798
  421.6 4.7 %update.1 = (f32[12,16,512]{2,1,0:T(8,128)}, f32[12,16,512]{2,1,0:T(8,128)}, f32[12,16,512]{2,1,0:T(8,128)}, bf16[12,16,512]{2,1,0:T(8,128)(2,1)}, f32[2,16,3200...) custom-call(f32[12,16,512]{2,1,0:T(8,128)} %refs_0_.1, ...), custom_call_target="tpu_custom_call" | custom-call | tf_op jit(solution)/shard_map/update/pallas_call | solution.py:745
  (319 shorter events, 109.6 us)
Async XLA Ops:
  7.3 117.2 %all-gather.5.cloned.1.call-start = ((), (), s32[]{:S(2)}) async-start(), calls=%async_computation.5 | async-start | bytes 6758400 | tf_op jit(solution)/shard_map/all_gather | solution.py:763
  10.5 13.6 %collective-permute-start.2 = (bf16[16,2432]{1,0:T(8,128)(2,1)S(1)}, bf16[16,2432]{1,0:T(8,128)(2,1)S(1)}, u32[]{:S(2)}, u32[]{:S(2)}) collective-permute-start(bf16[16,2432]{1,0:T(8,128)(2,1)S(1)} %concatenate.62), channel_id=1, source_target_pairs={{0,3},{1,2},{2,1},{3,0},{4,7},{5,6},{6,5},{7,4},{8,11},{9,10},{10,... | collective-permute-start | bytes 233480 | tf_op jit(solution)/shard_map/ppermute | solution.py:798
  17.4 55.0 %all-to-all-start = ((bf16[4,288,512]{2,1,0:T(8,128)(2,1)}), bf16[4,288,512]{2,1,0:T(8,128)(2,1)}, u32[]{:S(2)}, u32[]{:S(2)}) async-start(bf16[4,288,512]{2,1,0:T(8,128)(2,1)} %fusion.1), calls=%async_computation | async-start | bytes 2359296 | tf_op jit(solution)/shard_map/all_to_all | solution.py:864
  22.6 165.5 %all-gather.3.cloned.1.call-start = ((), (), s32[]{:S(2)}) async-start(), calls=%async_computation.4 | async-start | bytes 4325376 | tf_op jit(solution)/shard_map/all_gather | solution.py:763
  26.7 13.9 %collective-permute-start.4 = (bf16[64,2432]{1,0:T(8,128)(2,1)S(1)}, bf16[64,2432]{1,0:T(8,128)(2,1)S(1)}, u32[]{:S(2)}, u32[]{:S(2)}) collective-permute-start(bf16[64,2432]{1,0:T(8,128)(2,1)S(1)} %pad_maximum_fusion.5), channel_id=1, source_target_pairs={{0,16},{4,20},{8,24},{12,28},{16,0},{20,4},{24,8},{28,12},{1,17},{... | collective-permute-start | bytes 933896 | tf_op jit(solution)/shard_map/ppermute | solution.py:798
  43.9 70.5 %collective-permute-start.9 = (bf16[16,6400]{1,0:T(8,128)(2,1)}, bf16[16,6400]{1,0:T(8,128)(2,1)}, u32[]{:S(2)}, u32[]{:S(2)}) collective-permute-start(bf16[16,6400]{1,0:T(8,128)(2,1)} %pad_maximum_fusion.6), channel_id=1, source_target_pairs={{0,3},{1,2},{2,1},{3,0},{4,7},{5,6},{6,5},{7,4},{8,11},{9,10},{10,... | collective-permute-start | bytes 614408 | tf_op jit(solution)/shard_map/ppermute | solution.py:798
  47.5 67.0 %collective-permute-start.8 = (bf16[16,6400]{1,0:T(8,128)(2,1)}, bf16[16,6400]{1,0:T(8,128)(2,1)}, u32[]{:S(2)}, u32[]{:S(2)}) collective-permute-start(bf16[16,6400]{1,0:T(8,128)(2,1)} %pad_maximum_fusion.6), channel_id=1, source_target_pairs={{0,1},{1,0},{2,3},{3,2},{4,5},{5,4},{6,7},{7,6},{8,9},{9,8},{10,11... | collective-permute-start | bytes 614408 | tf_op jit(solution)/shard_map/ppermute | solution.py:798
  47.5 67.0 %collective-permute-start.7 = (bf16[16,6400]{1,0:T(8,128)(2,1)}, bf16[16,6400]{1,0:T(8,128)(2,1)}, u32[]{:S(2)}, u32[]{:S(2)}) collective-permute-start(bf16[16,6400]{1,0:T(8,128)(2,1)} %pad_maximum_fusion.6), channel_id=1, source_target_pairs={{0,2},{1,3},{2,0},{3,1},{4,6},{5,7},{6,4},{7,5},{8,10},{9,11},{10,... | collective-permute-start | bytes 614408 | tf_op jit(solution)/shard_map/ppermute | solution.py:798
  72.4 42.0 %all-to-all-start.1 = ((f32[4,32,128]{2,1,0:T(8,128)}), f32[4,32,128]{2,1,0:T(8,128)}, u32[]{:S(2)}, u32[]{:S(2)}) async-start(f32[4,32,128]{2,1,0:T(8,128)} %pad.123), calls=%async_computation.1 | async-start | bytes 131072 | tf_op jit(solution)/shard_map/all_to_all | solution.py:864
  120.4 27.3 %collective-permute-start.12 = (bf16[64,6400]{1,0:T(8,128)(2,1)}, bf16[64,6400]{1,0:T(8,128)(2,1)S(1)}, u32[]{:S(2)}, u32[]{:S(2)}) collective-permute-start(bf16[64,6400]{1,0:T(8,128)(2,1)} %get-tuple-element.415), channel_id=1, source_target_pairs={{0,24},{4,28},{8,16},{12,20},{16,8},{20,12},{24,0},{28,4},{1,25},{... | collective-permute-start | bytes 2457608 | tf_op jit(solution)/shard_map/ppermute | solution.py:798
  122.5 39.9 %collective-permute-start.11 = (bf16[64,6400]{1,0:T(8,128)(2,1)}, bf16[64,6400]{1,0:T(8,128)(2,1)S(1)}, u32[]{:S(2)}, u32[]{:S(2)}) collective-permute-start(bf16[64,6400]{1,0:T(8,128)(2,1)} %get-tuple-element.415), channel_id=1, source_target_pairs={{0,16},{4,20},{8,24},{12,28},{16,0},{20,4},{24,8},{28,12},{1,17},{... | collective-permute-start | bytes 2457608 | tf_op jit(solution)/shard_map/ppermute | solution.py:798
  123.3 43.7 %collective-permute-start.10 = (bf16[64,6400]{1,0:T(8,128)(2,1)}, bf16[64,6400]{1,0:T(8,128)(2,1)S(1)}, u32[]{:S(2)}, u32[]{:S(2)}) collective-permute-start(bf16[64,6400]{1,0:T(8,128)(2,1)} %get-tuple-element.415), channel_id=1, source_target_pairs={{0,8},{4,12},{8,0},{12,4},{16,24},{20,28},{24,16},{28,20},{1,9},{5... | collective-permute-start | bytes 2457608 | tf_op jit(solution)/shard_map/ppermute | solution.py:798
  223.6 138.4 %all-to-all-start.2 = ((bf16[4,32,512]{2,1,0:T(8,128)(2,1)}), bf16[4,32,512]{2,1,0:T(8,128)(2,1)}, u32[]{:S(2)}, u32[]{:S(2)}) async-start(bf16[4,32,512]{2,1,0:T(8,128)(2,1)} %bitcast.147), calls=%async_computation.2 | async-start | bytes 262144 | tf_op jit(solution)/shard_map/all_to_all | solution.py:864
  239.3 40.7 %collective-permute-start.18 = (bf16[64,6400]{1,0:T(8,128)(2,1)S(1)}, bf16[64,6400]{1,0:T(8,128)(2,1)}, u32[]{:S(2)}, u32[]{:S(2)}) collective-permute-start(bf16[64,6400]{1,0:T(8,128)(2,1)S(1)} %get-tuple-element.389), channel_id=1, source_target_pairs={{0,24},{4,28},{8,16},{12,20},{16,8},{20,12},{24,0},{28,4},{1,25},{... | collective-permute-start | bytes 2457608 | tf_op jit(solution)/shard_map/ppermute | solution.py:798
  241.2 38.8 %collective-permute-start.17 = (bf16[64,6400]{1,0:T(8,128)(2,1)S(1)}, bf16[64,6400]{1,0:T(8,128)(2,1)}, u32[]{:S(2)}, u32[]{:S(2)}) collective-permute-start(bf16[64,6400]{1,0:T(8,128)(2,1)S(1)} %get-tuple-element.390), channel_id=1, source_target_pairs={{0,16},{4,20},{8,24},{12,28},{16,0},{20,4},{24,8},{28,12},{1,17},{... | collective-permute-start | bytes 2457608 | tf_op jit(solution)/shard_map/ppermute | solution.py:798
  242.7 37.4 %collective-permute-start.16 = (bf16[64,6400]{1,0:T(8,128)(2,1)S(1)}, bf16[64,6400]{1,0:T(8,128)(2,1)}, u32[]{:S(2)}, u32[]{:S(2)}) collective-permute-start(bf16[64,6400]{1,0:T(8,128)(2,1)S(1)} %get-tuple-element.391), channel_id=1, source_target_pairs={{0,8},{4,12},{8,0},{12,4},{16,24},{20,28},{24,16},{28,20},{1,9},{5... | collective-permute-start | bytes 2457608 | tf_op jit(solution)/shard_map/ppermute | solution.py:798
  281.8 26.2 %collective-permute-start.19 = (bf16[256,6912]{1,0:T(8,128)(2,1)}, bf16[256,6912]{1,0:T(8,128)(2,1)}, u32[]{:S(2)}, u32[]{:S(2)}) collective-permute-start(bf16[256,6912]{1,0:T(8,128)(2,1)} %get-tuple-element.266), channel_id=1, source_target_pairs={{0,4},{4,0},{8,12},{12,8},{16,20},{20,16},{24,28},{28,24},{1,5},{5... | collective-permute-start | bytes 10616840 | tf_op jit(solution)/shard_map/ppermute | solution.py:798
  284.9 27.6 %collective-permute-start.20 = (bf16[32,6400]{1,0:T(8,128)(2,1)}, bf16[32,6400]{1,0:T(8,128)(2,1)}, u32[]{:S(2)}, u32[]{:S(2)}) collective-permute-start(bf16[32,6400]{1,0:T(8,128)(2,1)} %get-tuple-element.399), channel_id=1, source_target_pairs={{0,1},{1,0},{2,3},{3,2},{4,5},{5,4},{6,7},{7,6},{8,9},{9,8},{10,11... | collective-permute-start | bytes 1228808 | tf_op jit(solution)/shard_map/ppermute | solution.py:798
  290.1 22.4 %collective-permute-start.23 = (bf16[64,4096]{1,0:T(8,128)(2,1)}, bf16[64,4096]{1,0:T(8,128)(2,1)}, u32[]{:S(2)}, u32[]{:S(2)}) collective-permute-start(bf16[64,4096]{1,0:T(8,128)(2,1)} %get-tuple-element.393), channel_id=1, source_target_pairs={{0,24},{4,28},{8,16},{12,20},{16,8},{20,12},{24,0},{28,4},{1,25},{... | collective-permute-start | bytes 1572872 | tf_op jit(solution)/shard_map/ppermute | solution.py:798
  292.0 24.5 %collective-permute-start.22 = (bf16[64,4096]{1,0:T(8,128)(2,1)}, bf16[64,4096]{1,0:T(8,128)(2,1)}, u32[]{:S(2)}, u32[]{:S(2)}) collective-permute-start(bf16[64,4096]{1,0:T(8,128)(2,1)} %get-tuple-element.394), channel_id=1, source_target_pairs={{0,16},{4,20},{8,24},{12,28},{16,0},{20,4},{24,8},{28,12},{1,17},{... | collective-permute-start | bytes 1572872 | tf_op jit(solution)/shard_map/ppermute | solution.py:798
  293.4 23.1 %collective-permute-start.21 = (bf16[64,4096]{1,0:T(8,128)(2,1)}, bf16[64,4096]{1,0:T(8,128)(2,1)}, u32[]{:S(2)}, u32[]{:S(2)}) collective-permute-start(bf16[64,4096]{1,0:T(8,128)(2,1)} %get-tuple-element.395), channel_id=1, source_target_pairs={{0,8},{4,12},{8,0},{12,4},{16,24},{20,28},{24,16},{28,20},{1,9},{5... | collective-permute-start | bytes 1572872 | tf_op jit(solution)/shard_map/ppermute | solution.py:798
  317.5 29.5 %collective-permute-start.24 = (bf16[16,6400]{1,0:T(8,128)(2,1)S(1)}, bf16[16,6400]{1,0:T(8,128)(2,1)S(1)}, u32[]{:S(2)}, u32[]{:S(2)}) collective-permute-start(bf16[16,6400]{1,0:T(8,128)(2,1)S(1)} %add_convert_fusion.24), channel_id=1, source_target_pairs={{0,2},{1,3},{2,0},{3,1},{4,6},{5,7},{6,4},{7,5},{8,10},{9,11},{10,... | collective-permute-start | bytes 614408 | tf_op jit(solution)/shard_map/ppermute | solution.py:798
  321.6 25.4 %collective-permute-start.25 = (bf16[32,4096]{1,0:T(8,128)(2,1)S(1)}, bf16[32,4096]{1,0:T(8,128)(2,1)S(1)}, u32[]{:S(2)}, u32[]{:S(2)}) collective-permute-start(bf16[32,4096]{1,0:T(8,128)(2,1)S(1)} %get-tuple-element.405), channel_id=1, source_target_pairs={{0,1},{1,0},{2,3},{3,2},{4,5},{5,4},{6,7},{7,6},{8,9},{9,8},{10,11... | collective-permute-start | bytes 786440 | tf_op jit(solution)/shard_map/ppermute | solution.py:798
  322.2 39.9 %collective-permute-start.27 = (bf16[64,6912]{1,0:T(8,128)(2,1)}, bf16[64,6912]{1,0:T(8,128)(2,1)S(1)}, u32[]{:S(2)}, u32[]{:S(2)}) collective-permute-start(bf16[64,6912]{1,0:T(8,128)(2,1)} %get-tuple-element.301), channel_id=1, source_target_pairs={{0,8},{4,12},{8,0},{12,4},{16,24},{20,28},{24,16},{28,20},{1,9},{5... | collective-permute-start | bytes 2654216 | tf_op jit(solution)/shard_map/ppermute | solution.py:798
  323.1 38.9 %collective-permute-start.28 = (bf16[64,6912]{1,0:T(8,128)(2,1)}, bf16[64,6912]{1,0:T(8,128)(2,1)}, u32[]{:S(2)}, u32[]{:S(2)}) collective-permute-start(bf16[64,6912]{1,0:T(8,128)(2,1)} %get-tuple-element.302), channel_id=1, source_target_pairs={{0,16},{4,20},{8,24},{12,28},{16,0},{20,4},{24,8},{28,12},{1,17},{... | collective-permute-start | bytes 2654216 | tf_op jit(solution)/shard_map/ppermute | solution.py:798
  324.6 38.0 %collective-permute-start.29 = (bf16[64,6912]{1,0:T(8,128)(2,1)}, bf16[64,6912]{1,0:T(8,128)(2,1)}, u32[]{:S(2)}, u32[]{:S(2)}) collective-permute-start(bf16[64,6912]{1,0:T(8,128)(2,1)} %get-tuple-element.303), channel_id=1, source_target_pairs={{0,24},{4,28},{8,16},{12,20},{16,8},{20,12},{24,0},{28,4},{1,25},{... | collective-permute-start | bytes 2654216 | tf_op jit(solution)/shard_map/ppermute | solution.py:798
  348.2 13.9 %collective-permute-start.26 = (bf16[16,4096]{1,0:T(8,128)(2,1)S(1)}, bf16[16,4096]{1,0:T(8,128)(2,1)S(1)}, u32[]{:S(2)}, u32[]{:S(2)}) collective-permute-start(bf16[16,4096]{1,0:T(8,128)(2,1)S(1)} %add_convert_fusion.27), channel_id=1, source_target_pairs={{0,2},{1,3},{2,0},{3,1},{4,6},{5,7},{6,4},{7,5},{8,10},{9,11},{10,... | collective-permute-start | bytes 393224 | tf_op jit(solution)/shard_map/ppermute | solution.py:798
  369.9 39.9 %all-to-all-start.3 = ((bf16[4,256,512]{2,1,0:T(8,128)(2,1)}), bf16[4,256,512]{2,1,0:T(8,128)(2,1)S(1)}, u32[]{:S(2)}, u32[]{:S(2)}) async-start(bf16[4,256,512]{2,1,0:T(8,128)(2,1)} %bitcast.139), calls=%async_computation.3 | async-start | bytes 2097152 | tf_op jit(solution)/shard_map/all_to_all | solution.py:864
  379.5 30.3 %collective-permute-start.34 = (bf16[64,2048]{1,0:T(8,128)(2,1)S(1)}, bf16[64,2048]{1,0:T(8,128)(2,1)S(1)}, u32[]{:S(2)}, u32[]{:S(2)}) collective-permute-start(bf16[64,2048]{1,0:T(8,128)(2,1)S(1)} %get-tuple-element.401), channel_id=1, source_target_pairs={{0,24},{4,28},{8,16},{12,20},{16,8},{20,12},{24,0},{28,4},{1,25},{... | collective-permute-start | bytes 786440 | tf_op jit(solution)/shard_map/ppermute | solution.py:798
  380.4 29.5 %collective-permute-start.33 = (bf16[64,2048]{1,0:T(8,128)(2,1)S(1)}, bf16[64,2048]{1,0:T(8,128)(2,1)S(1)}, u32[]{:S(2)}, u32[]{:S(2)}) collective-permute-start(bf16[64,2048]{1,0:T(8,128)(2,1)S(1)} %get-tuple-element.402), channel_id=1, source_target_pairs={{0,16},{4,20},{8,24},{12,28},{16,0},{20,4},{24,8},{28,12},{1,17},{... | collective-permute-start | bytes 786440 | tf_op jit(solution)/shard_map/ppermute | solution.py:798
  382.2 27.7 %collective-permute-start.32 = (bf16[64,2048]{1,0:T(8,128)(2,1)S(1)}, bf16[64,2048]{1,0:T(8,128)(2,1)S(1)}, u32[]{:S(2)}, u32[]{:S(2)}) collective-permute-start(bf16[64,2048]{1,0:T(8,128)(2,1)S(1)} %get-tuple-element.403), channel_id=1, source_target_pairs={{0,8},{4,12},{8,0},{12,4},{16,24},{20,28},{24,16},{28,20},{1,9},{5... | collective-permute-start | bytes 786440 | tf_op jit(solution)/shard_map/ppermute | solution.py:798
  384.1 25.7 %collective-permute-start.35 = (bf16[16,6912]{1,0:T(8,128)(2,1)S(1)}, bf16[16,6912]{1,0:T(8,128)(2,1)S(1)}, u32[]{:S(2)}, u32[]{:S(2)}) collective-permute-start(bf16[16,6912]{1,0:T(8,128)(2,1)S(1)} %add_convert_fusion.23), channel_id=1, source_target_pairs={{0,2},{1,3},{2,0},{3,1},{4,6},{5,7},{6,4},{7,5},{8,10},{9,11},{10,... | collective-permute-start | bytes 663560 | tf_op jit(solution)/shard_map/ppermute | solution.py:798
  (70 other events, 897.6 us)
Sparse Core Ops, SparseCore 0:
  11.5 92.3 all-gather.4
  107.5 72.3 all-gather.2
where the time goes:
time: 441 us; the launch traced here: 436 us
  Pallas kernels  193 us (44%)
  waiting for transfers between devices  72.2 us (16%)
  starting transfers between devices  63.3 us (14%)
  local copies, waits for them, and re-layouts  47.2 us (11%)
  other arithmetic  42.9 us (10%)
  between operations  15.8 us (4%)
    ppermute x39, waiting for transfers between devices, exchange(): return lax.ppermute(values, axis, pairs)  71.9 us
    pallas_call x3, Pallas kernels, attend_back(): pl.pallas_call(functools.partial(attend_back_kernel, chunk=256, first=fir...  46.9 us
    ppermute x39, starting transfers between devices, exchange(): return lax.ppermute(values, axis, pairs)  44 us
    pallas_call x1, Pallas kernels, feed_back(): pl.pallas_call(functools.partial(backward_kernel, tile=256), grid=(steps,...  37.2 us
    pallas_call x1, Pallas kernels, decode(): pl.pallas_call(functools.partial(decode_kernel, spacing=spacing, joints=j...  34.9 us
    pallas_call x1, Pallas kernels, attend(): pl.pallas_call(functools.partial(attend_kernel, chunk=256), grid=(pairs,)...  33.3 us
    pallas_call x1, Pallas kernels, feed_forward(): pl.pallas_call(functools.partial(forward_kernel, tile=256), grid=(steps,)...  23.2 us
    convert_element_type x14, other arithmetic, to_half(): return values.astype(BF)  23.1 us
  transfers between devices with their start and end apart: 45, of which 12 were waited for; matrix products, arithmetic and copies ran while one was open for 15% of the time, Pallas kernels for 35%

commit v1 on v0

--- a/solution.py
+++ b/solution.py
@@ -155,7 +155,7 @@
     mats = [pl.BlockSpec((width, PAIR), lambda i, j=j: (0, i + j * pairs)) for j in range(3)]
     half = jax.ShapeDtypeStruct((rows, width), BF)
     return pl.pallas_call(
-        functools.partial(attend_kernel, chunk=256),
+        functools.partial(attend_kernel, chunk=512),
         grid=(pairs,),
         in_specs=[whole, whole] + mats + [pl.BlockSpec((vec.shape[0], PAIR), lambda i: (0, i))],
         out_specs=[own] * 4 + [pl.BlockSpec((1, 2, rows), lambda i: (i, 0, 0))],

time: 441 us -> 437 us (level)
  Pallas kernels: 193 us -> 184 us
  waiting for transfers between devices: 72.2 us -> 80.9 us
    all_gather x2, waiting for transfers between devices: 0.01 us -> 11 us  [gather(): return lax.all_gather(columns, ALL, axis=0, tiled=True)]
    pallas_call x1, Pallas kernels: 33.3 us -> 23.9 us  [attend(): pl.pallas_call(functools.partial(attend_kernel, chunk=512), grid=(pairs,)...]
  transfers between devices with their start and end apart: 45 -> 45, of which waited for: 12 -> 13; matrix products, arithmetic and copies ran while one was open for 15% -> 15% of each run, Pallas kernels for 35% -> 33%
where the time goes in v1:
time: 437 us; the launch traced here: 432 us
  Pallas kernels  184 us (42%)
  waiting for transfers between devices  80.9 us (19%)
  starting transfers between devices  60.6 us (14%)
  local copies, waits for them, and re-layouts  47.1 us (11%)
  other arithmetic  42.9 us (10%)
  between operations  15.8 us (4%)
    ppermute x39, waiting for transfers between devices, exchange(): return lax.ppermute(values, axis, pairs)  69.6 us
    pallas_call x3, Pallas kernels, attend_back(): pl.pallas_call(functools.partial(attend_back_kernel, chunk=256, first=fir...  46.9 us
    ppermute x39, starting transfers between devices, exchange(): return lax.ppermute(values, axis, pairs)  42.5 us
    pallas_call x1, Pallas kernels, feed_back(): pl.pallas_call(functools.partial(backward_kernel, tile=256), grid=(steps,...  37.2 us
    pallas_call x1, Pallas kernels, decode(): pl.pallas_call(functools.partial(decode_kernel, spacing=spacing, joints=j...  34.9 us
    pallas_call x1, Pallas kernels, attend(): pl.pallas_call(functools.partial(attend_kernel, chunk=512), grid=(pairs,)...  23.9 us
    pallas_call x1, Pallas kernels, feed_forward(): pl.pallas_call(functools.partial(forward_kernel, tile=256), grid=(steps,)...  23.2 us
    convert_element_type x14, other arithmetic, to_half(): return values.astype(BF)  23.1 us
  transfers between devices with their start and end apart: 45, of which 13 were waited for; matrix products, arithmetic and copies ran while one was open for 15% of the time, Pallas kernels for 33%

profile of v1, /device:TPU:0, one launch (start us, length us, event | category | flops | bytes accessed | tf_op | source)
XLA Modules:
  0.0 432.4 jit_solution(15436182361930378440)
XLA Ops:
  10.5 5.0 %collective-permute-start.2 = (bf16[16,2432]{1,0:T(8,128)(2,1)S(1)}, bf16[16,2432]{1,0:T(8,128)(2,1)S(1)}, u32[]{:S(2)}, u32[]{:S(2)}) collective-permute-start(bf16[16,2432]{1,0:T(8,128)(2,1)S(1)} %concatenate.62), channel_id=1, source_target_pairs={{0,3},{1,2},{2,1},{3,0},{4,7},{5,6},{6,5},{7,4},{8,11},{9,10},{10,... | collective-permute-start | bytes 233480 | tf_op jit(solution)/shard_map/ppermute | solution.py:798
  17.4 5.1 %all-to-all-start = ((bf16[4,288,512]{2,1,0:T(8,128)(2,1)}), bf16[4,288,512]{2,1,0:T(8,128)(2,1)}, u32[]{:S(2)}, u32[]{:S(2)}) async-start(bf16[4,288,512]{2,1,0:T(8,128)(2,1)} %fusion.1), calls=%async_computation | async-start | bytes 2359296 | tf_op jit(solution)/shard_map/all_to_all | solution.py:864
  24.2 2.5 collective-permute-start.5
  27.8 7.7 %collective-permute-done.5 = bf16[64,2432]{1,0:T(8,128)(2,1)S(1)} collective-permute-done((bf16[64,2432]{1,0:T(8,128)(2,1)S(1)}, bf16[64,2432]{1,0:T(8,128)(2,1)S(1)}, u32[]{:S(2)}, u32[]{:S(2)}) %collective-permute-start.5) | collective-permute-done | bytes 311328 | tf_op jit(solution)/shard_map/ppermute | solution.py:798
  35.4 5.2 %collective-permute-done.4 = bf16[64,2432]{1,0:T(8,128)(2,1)S(1)} collective-permute-done((bf16[64,2432]{1,0:T(8,128)(2,1)S(1)}, bf16[64,2432]{1,0:T(8,128)(2,1)S(1)}, u32[]{:S(2)}, u32[]{:S(2)}) %collective-permute-start.4) | collective-permute-done | bytes 311328 | tf_op jit(solution)/shard_map/ppermute | solution.py:798
  43.9 3.5 collective-permute-start.9
  72.4 4.9 %all-to-all-start.1 = ((f32[4,32,128]{2,1,0:T(8,128)}), f32[4,32,128]{2,1,0:T(8,128)}, u32[]{:S(2)}, u32[]{:S(2)}) async-start(f32[4,32,128]{2,1,0:T(8,128)} %pad.123), calls=%async_computation.1 | async-start | bytes 131072 | tf_op jit(solution)/shard_map/all_to_all | solution.py:864
  79.6 23.9 %attend.1 = (bf16[1024,512]{1,0:T(8,128)(2,1)}, bf16[1024,512]{1,0:T(8,128)(2,1)}, bf16[1024,512]{1,0:T(8,128)(2,1)}, bf16[1024,512]{1,0:T(8,128)(2,1)}, f32[4,2,1024]{2,1,0:T(2,128)}) custom-call(bf16[1024,512]{1,0:T(8,128)(2,1)} %bitcast.135, f32[1024,512]{1,0:T(8,128)} %constant.59.clone.pos_ref, bf16[512,2432]{1,0:T(8,128)(2,1)} %copy-done.4, ...), custom_call_target="tpu_custom_call" | custom-call | flops 8589934592 | bytes 6291456 | tf_op jit(solution)/shard_map/attend/pallas_call | solution.py:157
  115.1 23.2 %feed_forward.1 = (f32[1024,512]{1,0:T(8,128)}, bf16[1024,512]{1,0:T(8,128)(2,1)}, f32[1024,3200]{1,0:T(8,128)}, f32[1024,512]{1,0:T(8,128)}, f32[1024,512]{1,0:T(8,128)}) custom-call(bf16[1024,512]{1,0:T(8,128)(2,1)} %get-tuple-element.208.mixed_ref.o_ref, bf16[1024,512]{1,0:T(8,128)(2,1)} %bitcast.136, bf16[512,2432]{1,0:T(8,128)(2,1)} %copy-done.4, ...), custom_call_target="tpu_custom_call" | custom-call | flops 6710886400 | bytes 13107200 | tf_op jit(solution)/shard_map/feed_forward/pallas_call | solution.py:221
  138.3 14.0 %collective-permute-done.11 = bf16[64,6400]{1,0:T(8,128)(2,1)S(1)} collective-permute-done((bf16[64,6400]{1,0:T(8,128)(2,1)}, bf16[64,6400]{1,0:T(8,128)(2,1)S(1)}, u32[]{:S(2)}, u32[]{:S(2)}) %collective-permute-start.11) | collective-permute-done | bytes 819232 | tf_op jit(solution)/shard_map/ppermute | solution.py:798
  158.8 5.8 %collective-permute-done.13.bottom_ref = bf16[256,6400]{1,0:T(8,128)(2,1)S(1)} collective-permute-done((bf16[256,6400]{1,0:T(8,128)(2,1)S(1)}, bf16[256,6400]{1,0:T(8,128)(2,1)S(1)}, u32[]{:S(2)}, u32[]{:S(2)}) %collective-permute-start.13) | collective-permute-done | bytes 3276832 | tf_op jit(solution)/shard_map/ppermute | solution.py:798
  164.7 6.9 %settle.3.f_ref = bf16[512,6400]{1,0:T(8,128)(2,1)S(1)} custom-call(bf16[256,6400]{1,0:T(8,128)(2,1)S(1)} %constant_dynamic-update-slice_fusion.19.top_ref, bf16[256,6400]{1,0:T(8,128)(2,1)S(1)} %collective-permute-done.13.bottom_ref, bf16[512,512]{1,0:T(8,128)(2,1)S(1)} %get-tuple-element.436.turn_ref), custom_call_target="tpu_custom_call" | custom-call | flops 3355443200 | bytes 13107200 | tf_op jit(solution)/shard_map/settle/pallas_call | solution.py:108
  171.6 2.8 copy-done
  174.4 11.0 %all-gather.3.cloned.1.call-done.w_ref = bf16[512,4096]{1,0:T(8,128)(2,1)} async-done(((bf16[16,4096]{1,0:T(8,128)(2,1)}), bf16[512,4096]{1,0:T(8,128)(2,1)}) %all-gather.3.cloned.1.call-update) | async-done | bytes 4194320 | tf_op jit(solution)/shard_map/all_gather | solution.py:763
  185.3 34.9 %decode.1 = (bf16[256,4096]{1,0:T(8,128)(2,1)}, bf16[256,4096]{1,0:T(8,128)(2,1)}, bf16[256,6400]{1,0:T(8,128)(2,1)}, bf16[256,6400]{1,0:T(8,128)(2,1)}, bf16[12...) custom-call(bf16[128,512]{1,0:T(8,128)(2,1)} %bitcast.143, ...), custom_call_target="tpu_custom_call" | custom-call | flops 3221225472 | bytes 8388608 | tf_op jit(solution)/shard_map/decode/pallas_call | solution.py:686
  220.8 4.2 all-to-all-start.2
  231.7 3.6 add_convert_fusion.7
  238.8 37.2 %feed_back.1 = (bf16[256,6912]{1,0:T(8,128)(2,1)}, bf16[256,6912]{1,0:T(8,128)(2,1)}, f32[1024,512]{1,0:T(8,128)}, bf16[1024,512]{1,0:T(8,128)(2,1)}, f32[8,512]{1,0:T(8,128)}, /*index=5*/f32[1,3200]{1,0:T(1,128)}) custom-call(f32[1024,512]{1,0:T(8,128)} %copy-done.14, bf16[512,1024]{1,0:T(8,128)(2,1)} %copy-done.15, ...), custom_call_target="tpu_custom_call" | custom-call | flops 13421772800 | bytes 19660800 | tf_op jit(solution)/shard_map/feed_back/pallas_call | solution.py:375
  277.9 3.0 add_convert_fusion.15
  282.9 3.1 add_convert_fusion.8
  291.1 12.9 %attend_back.3 = (bf16[256,1536]{1,0:T(8,128)(2,1)}, bf16[256,1536]{1,0:T(8,128)(2,1)}, f32[1024,512]{1,0:T(8,128)}, f32[8,128]{1,0:T(8,128)}) custom-call(bf16[1024,512]{1,0:T(8,128)(2,1)} %get-tuple-element.254.q_ref, bf16[1024,512]{1,0:T(8,128)(2,1)} %get-tuple-element.255.k_ref, bf16[1024,512]{1,0:T(8,128)(2,1)} %get-tuple-element.256.v_ref, ...), custom_call_target="tpu_custom_call" | custom-call | flops 5368709120 | bytes 8388608 | tf_op jit(solution)/shard_map/attend_back/pallas_call | solution.py:482
  304.1 4.4 %add_convert_fusion = (bf16[64,6912]{1,0:T(8,128)(2,1)}, bf16[64,6912]{1,0:T(8,128)(2,1)}, bf16[64,6912]{1,0:T(8,128)(2,1)}, bf16[64,6912]{1,0:T(8,128)(2,1)}) fusion(bf16[256,6912]{1,0:T(8,128)(2,1)} %collective-permute-done.19, bf16[256,6912]{1,0:T(8,128)(2,1)S(1)} %copy-done.22), kind=kLoop, calls=%fused_computation.2 | loop fusion | flops 7077888 | bytes 10616832 | tf_op jit(solution)/shard_map/convert_element_type | solution.py:32
  308.5 3.9 collective-permute-done.22
  313.4 2.4 collective-permute-start.24
  321.6 21.3 %attend_back.4 = (bf16[256,1536]{1,0:T(8,128)(2,1)}, bf16[256,1536]{1,0:T(8,128)(2,1)}, f32[1024,512]{1,0:T(8,128)}, f32[8,256]{1,0:T(8,128)}) custom-call(bf16[1024,512]{1,0:T(8,128)(2,1)} %get-tuple-element.254.q_ref, bf16[1024,512]{1,0:T(8,128)(2,1)} %get-tuple-element.255.k_ref, bf16[1024,512]{1,0:T(8,128)(2,1)} %get-tuple-element.256.v_ref, ...), custom_call_target="tpu_custom_call" | custom-call | flops 10737418240 | bytes 8388608 | tf_op jit(solution)/shard_map/attend_back/pallas_call | solution.py:482
  344.5 12.7 %attend_back.5 = (bf16[256,1536]{1,0:T(8,128)(2,1)}, bf16[256,1536]{1,0:T(8,128)(2,1)}, bf16[1024,512]{1,0:T(8,128)(2,1)}, f32[8,128]{1,0:T(8,128)}) custom-call(bf16[1024,512]{1,0:T(8,128)(2,1)} %get-tuple-element.254.q_ref, bf16[1024,512]{1,0:T(8,128)(2,1)} %get-tuple-element.255.k_ref, bf16[1024,512]{1,0:T(8,128)(2,1)} %get-tuple-element.256.v_ref, ...), custom_call_target="tpu_custom_call" | custom-call | flops 5368709120 | bytes 8388608 | tf_op jit(solution)/shard_map/attend_back/pallas_call | solution.py:482
  361.1 2.7 add_convert_fusion.12
  366.5 3.8 all-to-all-start.3
  371.7 9.3 %collective-permute-done.30 = bf16[32,6912]{1,0:T(8,128)(2,1)} collective-permute-done((bf16[32,6912]{1,0:T(8,128)(2,1)}, bf16[32,6912]{1,0:T(8,128)(2,1)}, u32[]{:S(2)}, u32[]{:S(2)}) %collective-permute-start.30) | collective-permute-done | bytes 442400 | tf_op jit(solution)/shard_map/ppermute | solution.py:798
  381.6 3.4 collective-permute-start.32
  387.7 18.8 %collective-permute-done.35 = bf16[16,6912]{1,0:T(8,128)(2,1)S(1)} collective-permute-done((bf16[16,6912]{1,0:T(8,128)(2,1)S(1)}, bf16[16,6912]{1,0:T(8,128)(2,1)S(1)}, u32[]{:S(2)}, u32[]{:S(2)}) %collective-permute-start.35) | collective-permute-done | bytes 221216 | tf_op jit(solution)/shard_map/ppermute | solution.py:798
  418.1 4.7 %update.1 = (f32[12,16,512]{2,1,0:T(8,128)}, f32[12,16,512]{2,1,0:T(8,128)}, f32[12,16,512]{2,1,0:T(8,128)}, bf16[12,16,512]{2,1,0:T(8,128)(2,1)}, f32[2,16,3200...) custom-call(f32[12,16,512]{2,1,0:T(8,128)} %refs_0_.1, ...), custom_call_target="tpu_custom_call" | custom-call | tf_op jit(solution)/shard_map/update/pallas_call | solution.py:745
  (319 shorter events, 108.7 us)
Async XLA Ops:
  7.3 107.8 %all-gather.5.cloned.1.call-start = ((), (), s32[]{:S(2)}) async-start(), calls=%async_computation.5 | async-start | bytes 6758400 | tf_op jit(solution)/shard_map/all_gather | solution.py:763
  17.4 55.0 %all-to-all-start = ((bf16[4,288,512]{2,1,0:T(8,128)(2,1)}), bf16[4,288,512]{2,1,0:T(8,128)(2,1)}, u32[]{:S(2)}, u32[]{:S(2)}) async-start(bf16[4,288,512]{2,1,0:T(8,128)(2,1)} %fusion.1), calls=%async_computation | async-start | bytes 2359296 | tf_op jit(solution)/shard_map/all_to_all | solution.py:864
  22.6 162.7 %all-gather.3.cloned.1.call-start = ((), (), s32[]{:S(2)}) async-start(), calls=%async_computation.4 | async-start | bytes 4325376 | tf_op jit(solution)/shard_map/all_gather | solution.py:763
  26.7 13.9 %collective-permute-start.4 = (bf16[64,2432]{1,0:T(8,128)(2,1)S(1)}, bf16[64,2432]{1,0:T(8,128)(2,1)S(1)}, u32[]{:S(2)}, u32[]{:S(2)}) collective-permute-start(bf16[64,2432]{1,0:T(8,128)(2,1)S(1)} %pad_maximum_fusion.5), channel_id=1, source_target_pairs={{0,16},{4,20},{8,24},{12,28},{16,0},{20,4},{24,8},{28,12},{1,17},{... | collective-permute-start | bytes 933896 | tf_op jit(solution)/shard_map/ppermute | solution.py:798
  43.9 61.1 %collective-permute-start.9 = (bf16[16,6400]{1,0:T(8,128)(2,1)}, bf16[16,6400]{1,0:T(8,128)(2,1)}, u32[]{:S(2)}, u32[]{:S(2)}) collective-permute-start(bf16[16,6400]{1,0:T(8,128)(2,1)} %pad_maximum_fusion.6), channel_id=1, source_target_pairs={{0,3},{1,2},{2,1},{3,0},{4,7},{5,6},{6,5},{7,4},{8,11},{9,10},{10,... | collective-permute-start | bytes 614408 | tf_op jit(solution)/shard_map/ppermute | solution.py:798
  47.5 57.6 %collective-permute-start.8 = (bf16[16,6400]{1,0:T(8,128)(2,1)}, bf16[16,6400]{1,0:T(8,128)(2,1)}, u32[]{:S(2)}, u32[]{:S(2)}) collective-permute-start(bf16[16,6400]{1,0:T(8,128)(2,1)} %pad_maximum_fusion.6), channel_id=1, source_target_pairs={{0,1},{1,0},{2,3},{3,2},{4,5},{5,4},{6,7},{7,6},{8,9},{9,8},{10,11... | collective-permute-start | bytes 614408 | tf_op jit(solution)/shard_map/ppermute | solution.py:798
  47.5 57.6 %collective-permute-start.7 = (bf16[16,6400]{1,0:T(8,128)(2,1)}, bf16[16,6400]{1,0:T(8,128)(2,1)}, u32[]{:S(2)}, u32[]{:S(2)}) collective-permute-start(bf16[16,6400]{1,0:T(8,128)(2,1)} %pad_maximum_fusion.6), channel_id=1, source_target_pairs={{0,2},{1,3},{2,0},{3,1},{4,6},{5,7},{6,4},{7,5},{8,10},{9,11},{10,... | collective-permute-start | bytes 614408 | tf_op jit(solution)/shard_map/ppermute | solution.py:798
  72.4 32.7 %all-to-all-start.1 = ((f32[4,32,128]{2,1,0:T(8,128)}), f32[4,32,128]{2,1,0:T(8,128)}, u32[]{:S(2)}, u32[]{:S(2)}) async-start(f32[4,32,128]{2,1,0:T(8,128)} %pad.123), calls=%async_computation.1 | async-start | bytes 131072 | tf_op jit(solution)/shard_map/all_to_all | solution.py:864
  111.0 27.3 %collective-permute-start.12 = (bf16[64,6400]{1,0:T(8,128)(2,1)}, bf16[64,6400]{1,0:T(8,128)(2,1)S(1)}, u32[]{:S(2)}, u32[]{:S(2)}) collective-permute-start(bf16[64,6400]{1,0:T(8,128)(2,1)} %get-tuple-element.415), channel_id=1, source_target_pairs={{0,24},{4,28},{8,16},{12,20},{16,8},{20,12},{24,0},{28,4},{1,25},{... | collective-permute-start | bytes 2457608 | tf_op jit(solution)/shard_map/ppermute | solution.py:798
  113.2 39.1 %collective-permute-start.11 = (bf16[64,6400]{1,0:T(8,128)(2,1)}, bf16[64,6400]{1,0:T(8,128)(2,1)S(1)}, u32[]{:S(2)}, u32[]{:S(2)}) collective-permute-start(bf16[64,6400]{1,0:T(8,128)(2,1)} %get-tuple-element.415), channel_id=1, source_target_pairs={{0,16},{4,20},{8,24},{12,28},{16,0},{20,4},{24,8},{28,12},{1,17},{... | collective-permute-start | bytes 2457608 | tf_op jit(solution)/shard_map/ppermute | solution.py:798
  113.9 39.3 %collective-permute-start.10 = (bf16[64,6400]{1,0:T(8,128)(2,1)}, bf16[64,6400]{1,0:T(8,128)(2,1)S(1)}, u32[]{:S(2)}, u32[]{:S(2)}) collective-permute-start(bf16[64,6400]{1,0:T(8,128)(2,1)} %get-tuple-element.415), channel_id=1, source_target_pairs={{0,8},{4,12},{8,0},{12,4},{16,24},{20,28},{24,16},{28,20},{1,9},{5... | collective-permute-start | bytes 2457608 | tf_op jit(solution)/shard_map/ppermute | solution.py:798
  220.8 137.2 %all-to-all-start.2 = ((bf16[4,32,512]{2,1,0:T(8,128)(2,1)}), bf16[4,32,512]{2,1,0:T(8,128)(2,1)}, u32[]{:S(2)}, u32[]{:S(2)}) async-start(bf16[4,32,512]{2,1,0:T(8,128)(2,1)} %bitcast.147), calls=%async_computation.2 | async-start | bytes 262144 | tf_op jit(solution)/shard_map/all_to_all | solution.py:864
  235.3 40.7 %collective-permute-start.18 = (bf16[64,6400]{1,0:T(8,128)(2,1)S(1)}, bf16[64,6400]{1,0:T(8,128)(2,1)}, u32[]{:S(2)}, u32[]{:S(2)}) collective-permute-start(bf16[64,6400]{1,0:T(8,128)(2,1)S(1)} %get-tuple-element.389), channel_id=1, source_target_pairs={{0,24},{4,28},{8,16},{12,20},{16,8},{20,12},{24,0},{28,4},{1,25},{... | collective-permute-start | bytes 2457608 | tf_op jit(solution)/shard_map/ppermute | solution.py:798
  236.7 39.4 %collective-permute-start.17 = (bf16[64,6400]{1,0:T(8,128)(2,1)S(1)}, bf16[64,6400]{1,0:T(8,128)(2,1)}, u32[]{:S(2)}, u32[]{:S(2)}) collective-permute-start(bf16[64,6400]{1,0:T(8,128)(2,1)S(1)} %get-tuple-element.390), channel_id=1, source_target_pairs={{0,16},{4,20},{8,24},{12,28},{16,0},{20,4},{24,8},{28,12},{1,17},{... | collective-permute-start | bytes 2457608 | tf_op jit(solution)/shard_map/ppermute | solution.py:798
  237.9 38.1 %collective-permute-start.16 = (bf16[64,6400]{1,0:T(8,128)(2,1)S(1)}, bf16[64,6400]{1,0:T(8,128)(2,1)}, u32[]{:S(2)}, u32[]{:S(2)}) collective-permute-start(bf16[64,6400]{1,0:T(8,128)(2,1)S(1)} %get-tuple-element.391), channel_id=1, source_target_pairs={{0,8},{4,12},{8,0},{12,4},{16,24},{20,28},{24,16},{28,20},{1,9},{5... | collective-permute-start | bytes 2457608 | tf_op jit(solution)/shard_map/ppermute | solution.py:798
  277.8 26.2 %collective-permute-start.19 = (bf16[256,6912]{1,0:T(8,128)(2,1)}, bf16[256,6912]{1,0:T(8,128)(2,1)}, u32[]{:S(2)}, u32[]{:S(2)}) collective-permute-start(bf16[256,6912]{1,0:T(8,128)(2,1)} %get-tuple-element.266), channel_id=1, source_target_pairs={{0,4},{4,0},{8,12},{12,8},{16,20},{20,16},{24,28},{28,24},{1,5},{5... | collective-permute-start | bytes 10616840 | tf_op jit(solution)/shard_map/ppermute | solution.py:798
  280.9 27.5 %collective-permute-start.20 = (bf16[32,6400]{1,0:T(8,128)(2,1)}, bf16[32,6400]{1,0:T(8,128)(2,1)}, u32[]{:S(2)}, u32[]{:S(2)}) collective-permute-start(bf16[32,6400]{1,0:T(8,128)(2,1)} %get-tuple-element.399), channel_id=1, source_target_pairs={{0,1},{1,0},{2,3},{3,2},{4,5},{5,4},{6,7},{7,6},{8,9},{9,8},{10,11... | collective-permute-start | bytes 1228808 | tf_op jit(solution)/shard_map/ppermute | solution.py:798
  286.1 22.4 %collective-permute-start.23 = (bf16[64,4096]{1,0:T(8,128)(2,1)}, bf16[64,4096]{1,0:T(8,128)(2,1)}, u32[]{:S(2)}, u32[]{:S(2)}) collective-permute-start(bf16[64,4096]{1,0:T(8,128)(2,1)} %get-tuple-element.393), channel_id=1, source_target_pairs={{0,24},{4,28},{8,16},{12,20},{16,8},{20,12},{24,0},{28,4},{1,25},{... | collective-permute-start | bytes 1572872 | tf_op jit(solution)/shard_map/ppermute | solution.py:798
  287.4 25.0 %collective-permute-start.22 = (bf16[64,4096]{1,0:T(8,128)(2,1)}, bf16[64,4096]{1,0:T(8,128)(2,1)}, u32[]{:S(2)}, u32[]{:S(2)}) collective-permute-start(bf16[64,4096]{1,0:T(8,128)(2,1)} %get-tuple-element.394), channel_id=1, source_target_pairs={{0,16},{4,20},{8,24},{12,28},{16,0},{20,4},{24,8},{28,12},{1,17},{... | collective-permute-start | bytes 1572872 | tf_op jit(solution)/shard_map/ppermute | solution.py:798
  288.6 23.8 %collective-permute-start.21 = (bf16[64,4096]{1,0:T(8,128)(2,1)}, bf16[64,4096]{1,0:T(8,128)(2,1)}, u32[]{:S(2)}, u32[]{:S(2)}) collective-permute-start(bf16[64,4096]{1,0:T(8,128)(2,1)} %get-tuple-element.395), channel_id=1, source_target_pairs={{0,8},{4,12},{8,0},{12,4},{16,24},{20,28},{24,16},{28,20},{1,9},{5... | collective-permute-start | bytes 1572872 | tf_op jit(solution)/shard_map/ppermute | solution.py:798
  313.4 29.5 %collective-permute-start.24 = (bf16[16,6400]{1,0:T(8,128)(2,1)S(1)}, bf16[16,6400]{1,0:T(8,128)(2,1)S(1)}, u32[]{:S(2)}, u32[]{:S(2)}) collective-permute-start(bf16[16,6400]{1,0:T(8,128)(2,1)S(1)} %add_convert_fusion.24), channel_id=1, source_target_pairs={{0,2},{1,3},{2,0},{3,1},{4,6},{5,7},{6,4},{7,5},{8,10},{9,11},{10,... | collective-permute-start | bytes 614408 | tf_op jit(solution)/shard_map/ppermute | solution.py:798
  317.5 25.4 %collective-permute-start.25 = (bf16[32,4096]{1,0:T(8,128)(2,1)S(1)}, bf16[32,4096]{1,0:T(8,128)(2,1)S(1)}, u32[]{:S(2)}, u32[]{:S(2)}) collective-permute-start(bf16[32,4096]{1,0:T(8,128)(2,1)S(1)} %get-tuple-element.405), channel_id=1, source_target_pairs={{0,1},{1,0},{2,3},{3,2},{4,5},{5,4},{6,7},{7,6},{8,9},{9,8},{10,11... | collective-permute-start | bytes 786440 | tf_op jit(solution)/shard_map/ppermute | solution.py:798
  318.1 39.9 %collective-permute-start.27 = (bf16[64,6912]{1,0:T(8,128)(2,1)}, bf16[64,6912]{1,0:T(8,128)(2,1)S(1)}, u32[]{:S(2)}, u32[]{:S(2)}) collective-permute-start(bf16[64,6912]{1,0:T(8,128)(2,1)} %get-tuple-element.301), channel_id=1, source_target_pairs={{0,8},{4,12},{8,0},{12,4},{16,24},{20,28},{24,16},{28,20},{1,9},{5... | collective-permute-start | bytes 2654216 | tf_op jit(solution)/shard_map/ppermute | solution.py:798
  319.2 38.8 %collective-permute-start.28 = (bf16[64,6912]{1,0:T(8,128)(2,1)}, bf16[64,6912]{1,0:T(8,128)(2,1)}, u32[]{:S(2)}, u32[]{:S(2)}) collective-permute-start(bf16[64,6912]{1,0:T(8,128)(2,1)} %get-tuple-element.302), channel_id=1, source_target_pairs={{0,16},{4,20},{8,24},{12,28},{16,0},{20,4},{24,8},{28,12},{1,17},{... | collective-permute-start | bytes 2654216 | tf_op jit(solution)/shard_map/ppermute | solution.py:798
  320.0 39.2 %collective-permute-start.29 = (bf16[64,6912]{1,0:T(8,128)(2,1)}, bf16[64,6912]{1,0:T(8,128)(2,1)}, u32[]{:S(2)}, u32[]{:S(2)}) collective-permute-start(bf16[64,6912]{1,0:T(8,128)(2,1)} %get-tuple-element.303), channel_id=1, source_target_pairs={{0,24},{4,28},{8,16},{12,20},{16,8},{20,12},{24,0},{28,4},{1,25},{... | collective-permute-start | bytes 2654216 | tf_op jit(solution)/shard_map/ppermute | solution.py:798
  363.8 17.3 %collective-permute-start.30 = (bf16[32,6912]{1,0:T(8,128)(2,1)}, bf16[32,6912]{1,0:T(8,128)(2,1)}, u32[]{:S(2)}, u32[]{:S(2)}) collective-permute-start(bf16[32,6912]{1,0:T(8,128)(2,1)} %get-tuple-element.397), channel_id=1, source_target_pairs={{0,1},{1,0},{2,3},{3,2},{4,5},{5,4},{6,7},{7,6},{8,9},{9,8},{10,11... | collective-permute-start | bytes 1327112 | tf_op jit(solution)/shard_map/ppermute | solution.py:798
  366.4 14.6 %collective-permute-start.31 = (bf16[256,2048]{1,0:T(8,128)(2,1)}, bf16[256,2048]{1,0:T(8,128)(2,1)S(1)}, u32[]{:S(2)}, u32[]{:S(2)}) collective-permute-start(bf16[256,2048]{1,0:T(8,128)(2,1)} %pad_maximum_fusion.1), channel_id=1, source_target_pairs={{0,4},{4,0},{8,12},{12,8},{16,20},{20,16},{24,28},{28,24},{1,5},{5... | collective-permute-start | bytes 3145736 | tf_op jit(solution)/shard_map/ppermute | solution.py:798
  366.5 39.9 %all-to-all-start.3 = ((bf16[4,256,512]{2,1,0:T(8,128)(2,1)}), bf16[4,256,512]{2,1,0:T(8,128)(2,1)S(1)}, u32[]{:S(2)}, u32[]{:S(2)}) async-start(bf16[4,256,512]{2,1,0:T(8,128)(2,1)} %bitcast.139), calls=%async_computation.3 | async-start | bytes 2097152 | tf_op jit(solution)/shard_map/all_to_all | solution.py:864
  381.4 25.0 %collective-permute-start.34 = (bf16[64,2048]{1,0:T(8,128)(2,1)S(1)}, bf16[64,2048]{1,0:T(8,128)(2,1)S(1)}, u32[]{:S(2)}, u32[]{:S(2)}) collective-permute-start(bf16[64,2048]{1,0:T(8,128)(2,1)S(1)} %get-tuple-element.401), channel_id=1, source_target_pairs={{0,24},{4,28},{8,16},{12,20},{16,8},{20,12},{24,0},{28,4},{1,25},{... | collective-permute-start | bytes 786440 | tf_op jit(solution)/shard_map/ppermute | solution.py:798
  381.5 24.9 %collective-permute-start.33 = (bf16[64,2048]{1,0:T(8,128)(2,1)S(1)}, bf16[64,2048]{1,0:T(8,128)(2,1)S(1)}, u32[]{:S(2)}, u32[]{:S(2)}) collective-permute-start(bf16[64,2048]{1,0:T(8,128)(2,1)S(1)} %get-tuple-element.402), channel_id=1, source_target_pairs={{0,16},{4,20},{8,24},{12,28},{16,0},{20,4},{24,8},{28,12},{1,17},{... | collective-permute-start | bytes 786440 | tf_op jit(solution)/shard_map/ppermute | solution.py:798
  381.6 24.9 %collective-permute-start.32 = (bf16[64,2048]{1,0:T(8,128)(2,1)S(1)}, bf16[64,2048]{1,0:T(8,128)(2,1)S(1)}, u32[]{:S(2)}, u32[]{:S(2)}) collective-permute-start(bf16[64,2048]{1,0:T(8,128)(2,1)S(1)} %get-tuple-element.403), channel_id=1, source_target_pairs={{0,8},{4,12},{8,0},{12,4},{16,24},{20,28},{24,16},{28,20},{1,9},{5... | collective-permute-start | bytes 786440 | tf_op jit(solution)/shard_map/ppermute | solution.py:798
  385.9 20.5 %collective-permute-start.35 = (bf16[16,6912]{1,0:T(8,128)(2,1)S(1)}, bf16[16,6912]{1,0:T(8,128)(2,1)S(1)}, u32[]{:S(2)}, u32[]{:S(2)}) collective-permute-start(bf16[16,6912]{1,0:T(8,128)(2,1)S(1)} %add_convert_fusion.23), channel_id=1, source_target_pairs={{0,2},{1,3},{2,0},{3,1},{4,6},{5,7},{6,4},{7,5},{8,10},{9,11},{10,... | collective-permute-start | bytes 663560 | tf_op jit(solution)/shard_map/ppermute | solution.py:798
  (70 other events, 863.7 us)
Sparse Core Ops, SparseCore 0:
  11.5 92.3 all-gather.4
  107.5 77.7 all-gather.2
